TPU v7x, 256 devices: a whole 4x4x8 slice. The times are simulated.
256 devices in a mesh: tile: 128 (over y, z, x), slab: 2 (over core).
Axes of the slice: x: 4, y: 4, z: 8, core: 2. Of those that a mesh axis runs over, the one named last changes fastest.
Arguments:
- amplitudes: float32 [128, 256, 1600], P('tile', None, 'slab'), may hold values from -6 to 6
- integrals: float32 [8192, 40, 1600], P('tile', None, 'slab'), may hold values from -0.02734375 to 0.02734375
- tile_map: int32 [128], replicated, may hold values from 0 to 127, each once
- cd_ids: int32 [8192], P('tile'), may hold values from 0 to 127, as said below
- res_ids: int32 [8192], P('tile'), may hold values from 0 to 1
Outputs:
- residual: float32 [256, 40, 256], P('tile', None, 'slab')
Inputs may be any that keep to these rules, and one draw needn't show every extreme that they name: `cd_ids`: the 64 entries of each aligned block of 64 name different amplitude tiles; one amplitude tile is named in every block.
All inputs are finite; a program needn't handle non-finite values.
Results may differ from a plain program's by a relative error of at most 0.0003.
Values sent between devices are 32-bit elements; how exact they have to be, the bound alone decides.
No kernel may reach another device: no remote copies, remote signals or barrier semaphores. Data moves between devices by JAX's collectives and lax.ppermute only.
A program may use at most 128 MiB of HBM per device.

v0:
```python
import jax
import jax.numpy as jnp
from jax import lax
from jax.sharding import PartitionSpec as P

RD = 2


def body(amplitudes, integrals, tile_map, cd_ids, res_ids):
    peer_count = lax.axis_size("tile")
    held_count = cd_ids.shape[0]
    positions = jnp.arange(peer_count, dtype=jnp.int32)
    matches = tile_map[None, :] == cd_ids[:, None]
    owner_slot = jnp.sum(jnp.where(matches, positions[None, :], 0), axis=1)
    routing = owner_slot[None, :] == positions[:, None]
    filled = jnp.any(routing, axis=1)
    picked = jnp.sum(
        jnp.where(routing, jnp.arange(held_count, dtype=jnp.int32)[None, :], 0), axis=1
    )
    outgoing = jnp.where(filled[:, None, None], integrals[picked], 0.0)
    own_tile = amplitudes[0]
    partials = jnp.einsum(
        "qav,rv->qar",
        lax.all_to_all(outgoing, "tile", split_axis=0, concat_axis=0, tiled=True),
        own_tile,
        precision=lax.Precision.HIGHEST,
    )
    select = (res_ids[None, :] == jnp.arange(RD, dtype=jnp.int32)[:, None]).astype(jnp.float32)
    weight = jnp.dot(select, routing.astype(jnp.float32).T, precision=lax.Precision.HIGHEST)
    returned = lax.all_to_all(partials, "tile", split_axis=0, concat_axis=0, tiled=True)
    summed = jnp.einsum("tp,par->tar", weight, returned, precision=lax.Precision.HIGHEST)
    return lax.psum_scatter(summed, "slab", scatter_dimension=2, tiled=True)


def solution(mesh):
    placed = (P("tile", None, "slab"), P("tile", None, "slab"), P(), P("tile"), P("tile"))
    return jax.shard_map(
        body, mesh=mesh, in_specs=placed, out_specs=P("tile", None, "slab"), check_vma=False
    )
```

profile of v0, /device:TPU:1, one launch (start us, length us, event | category | flops | bytes accessed | tf_op | source)
XLA Modules:
  0.0 623.3 jit_solution(11675912652251016411)
XLA Ops:
  6.5 0.0 copy-start
  6.5 0.9 select_reduce_fusion.1
  7.5 0.1 select_reduce_fusion
  7.6 0.1 fusion.4
  7.7 14.2 %gather_fusion = f32[128,40,800]{2,1,0:T(8,128)} fusion(f32[64,40,800]{2,1,0:T(8,128)} %param.6, s32[1024]{0:T(1024)S(1)} %pad_clamp_fusion), kind=kCustom, calls=%fused_computation | custom fusion | bytes 32768512 | tf_op jit(solution)/shard_map/gather | solution.py:20
  21.9 7.1 %broadcast_select_fusion = f32[128,40,800]{2,1,0:T(8,128)S(1)} fusion(f32[128,40,800]{2,1,0:T(8,128)} %gather_fusion, pred[128]{0:T(512)(128)(4,1)S(1)} %fusion.4), kind=kLoop, calls=%fused_computation.1 | loop fusion | flops 4096000 | bytes 32768128 | tf_op jit(solution)/shard_map/jit(_where)/select_n | solution.py:20
  29.0 414.0 %all_to_all.10 = f32[128,40,800]{2,1,0:T(8,128)S(1)} all-to-all(f32[128,40,800]{2,1,0:T(8,128)S(1)} %broadcast_select_fusion), channel_id=1, replica_groups=mesh['tile'=128,'slab'=2] {'tile'}, dimensions={0} | all-to-all | bytes 32768000 | tf_op jit(solution)/shard_map/all_to_all | solution.py:24
  443.0 0.0 copy-done
  443.0 0.0 copy-start.1
  443.0 18.7 %fusion.2 = f32[128,40,256]{2,1,0:T(8,128)} fusion(f32[128,40,800]{2,1,0:T(8,128)S(1)} %all_to_all.10, f32[1,256,800]{1,2,0:T(8,128)S(1)} %copy-done), kind=kOutput, calls=%fused_computation.5 | convolution fusion | flops 12582912000 | bytes 22446080 | tf_op jit(solution)/shard_map/qav,rv->qar/dot_general | solution.py:22
  461.7 9.9 %all-to-all-start.1 = ((f32[128,40,256]{2,1,0:T(8,128)}), f32[128,40,256]{2,1,0:T(8,128)}, u32[]{:S(2)}, u32[]{:S(2)}) async-start(f32[128,40,256]{2,1,0:T(8,128)} %fusion.2), calls=%async_computation.1 | async-start | bytes 10485760 | tf_op jit(solution)/shard_map/all_to_all | solution.py:30
  471.6 0.0 reduce-scatter.4.cloned.1.call-start
  471.6 0.0 copy-done.1
  471.6 0.2 convolution_bitcast_fusion
  471.8 114.8 %all-to-all-done.1 = f32[128,40,256]{2,1,0:T(8,128)} async-done(((f32[128,40,256]{2,1,0:T(8,128)}), f32[128,40,256]{2,1,0:T(8,128)}, u32[]{:S(2)}, u32[]{:S(2)}) %all-to-all-start.1) | async-done | bytes 5242912 | tf_op jit(solution)/shard_map/all_to_all | solution.py:30
  586.6 6.4 %fusion = f32[2,40,256]{2,0,1:T(2,128)S(1)} fusion(f32[2,128,1]{1,0,2:T(2,128)S(1)} %convolution_bitcast_fusion, f32[128,40,256]{2,1,0:T(8,128)} %all-to-all-done.1), kind=kOutput, calls=%fused_computation.2 | convolution fusion | flops 31457280 | bytes 5325824 | tf_op jit(solution)/shard_map/tp,par->tar/dot_general | solution.py:31
  593.0 3.2 copy.11
  596.2 4.4 reshape.28
  600.5 0.0 reduce-scatter.4.cloned.1.call-update
  600.6 12.8 %reduce-scatter.4.cloned.1.call-done = f32[128,80]{1,0:T(8,128)} async-done(((f32[256,80]{1,0:T(8,128)}), f32[128,80]{1,0:T(8,128)}) %reduce-scatter.4.cloned.1.call-update) | async-done | bytes 40976
  613.4 1.7 reshape.29
  615.0 1.4 copy.10
  (2 shorter events, 0.0 us)
Async XLA Ops:
  6.5 436.5 %copy-start = (f32[1,256,800]{1,2,0:T(8,128)S(1)}, f32[1,256,800]{1,2,0:T(8,128)}, u32[]{:S(2)}) copy-start(f32[1,256,800]{1,2,0:T(8,128)} %param.5) | copy-start | bytes 2457604
  443.0 28.6 %copy-start.1 = (s32[64]{0:T(128)S(1)}, s32[64]{0:T(128)}, u32[]{:S(2)}) copy-start(s32[64]{0:T(128)} %param.9) | copy-start | bytes 772
  461.7 124.9 %all-to-all-start.1 = ((f32[128,40,256]{2,1,0:T(8,128)}), f32[128,40,256]{2,1,0:T(8,128)}, u32[]{:S(2)}, u32[]{:S(2)}) async-start(f32[128,40,256]{2,1,0:T(8,128)} %fusion.2), calls=%async_computation.1 | async-start | bytes 10485760 | tf_op jit(solution)/shard_map/all_to_all | solution.py:30
  471.6 141.8 %reduce-scatter.4.cloned.1.call-start = ((), (), s32[]{:S(2)}) async-start(), calls=%async_computation.3 | async-start | bytes 196608
Sparse Core Ops, SparseCore 0:
  600.7 12.6 reduce-scatter.3
where the time goes:
time: 624 us; the launch traced here: 623 us
  blocking collectives  414 us (66%)
  waiting for transfers between devices  128 us (21%)
  matrix products  25.3 us (4%)
  local copies, waits for them, and re-layouts  24.8 us (4%)
  between operations  13.5 us (2%)
  starting transfers between devices  9.91 us (2%)
  other arithmetic  8.23 us (1%)
    all_to_all x1, blocking collectives, body(): lax.all_to_all(outgoing, 'tile', split_axis=0, concat_axis=0, tiled=True)  414 us
    all_to_all x1, waiting for transfers between devices, body(): lax.all_to_all(partials, 'tile', split_axis=0, concat_axis=0, tiled=True)  115 us
    dot_general x1, matrix products, body(): jnp.einsum('qav,rv->qar', lax.all_to_all(outgoing, 'tile', split_axis=0,...  18.7 us
    gather x1, local copies, waits for them, and re-layouts, body(): outgoing = jnp.where(filled[:, None, None], integrals[picked], 0.0)  14.2 us
    unnamed x2, waiting for transfers between devices  12.8 us
  transfers between devices with their start and end apart: 2, of which 2 were waited for; matrix products, arithmetic and copies ran while one was open for 0% of the time, Pallas kernels for 0%

commit v1 on v0

v1 whole, which is shorter than its diff:
```python
import jax
import jax.numpy as jnp
from jax import lax
from jax.sharding import Mesh, PartitionSpec as P

RD = 2
PLANE = ("y", "x")
TILE = ("y", "z", "x")


def body(amplitudes, integrals, tile_map, cd_ids, res_ids):
    cell = lax.axis_size(PLANE)
    tiles, rows, depth = integrals.shape
    wide = amplitudes.shape[1]
    part = depth // cell
    peers = tile_map.shape[0]
    positions = jnp.arange(peers, dtype=jnp.int32)
    owner = jnp.sum(jnp.where(tile_map[None, :] == cd_ids[:, None], positions[None, :], 0), axis=1)
    meta = lax.all_gather(jnp.stack([owner, res_ids]), PLANE)
    owners, targets = meta[:, 0], meta[:, 1]
    own = amplitudes[0].reshape(wide, cell, part).transpose(1, 2, 0)
    own = lax.all_to_all(own, PLANE, split_axis=0, concat_axis=0, tiled=True)
    held = lax.all_gather(own, "z")
    held = held.reshape(lax.axis_size("z"), lax.axis_size("y"), lax.axis_size("x"), part, wide)
    held = held.transpose(1, 0, 2, 3, 4).reshape(peers, part, wide)
    sent = integrals.reshape(tiles, rows, cell, part).transpose(2, 1, 0, 3).reshape(cell, rows, tiles * part)
    got = lax.all_to_all(sent, PLANE, split_axis=0, concat_axis=0, tiled=True)
    def one(block):
        own_rows, own_targets, block_v = block
        picked = held[own_rows].reshape(tiles * part, wide)
        select = own_targets[None, :] == jnp.arange(RD, dtype=jnp.int32)[:, None]
        select = jnp.repeat(select, part, axis=1)
        masked = jnp.where(select[:, None, :], block_v[None], 0.0).reshape(RD * rows, tiles * part)
        return jnp.dot(masked, picked, precision=lax.Precision.HIGHEST)

    sums = lax.map(one, (owners, targets, got))
    cores = lax.axis_size("slab")
    sums = sums.reshape(cell, RD * rows, cores, wide // cores).transpose(0, 2, 1, 3)
    sums = sums.reshape(cell * cores, RD * rows, wide // cores)
    back = lax.all_to_all(sums, PLANE + ("slab",), split_axis=0, concat_axis=0, tiled=True)
    return jnp.sum(back, axis=0).reshape(RD, rows, wide // cores)


def solution(mesh):
    grid = Mesh(mesh.devices.reshape(4, 8, 4, 2), ("y", "z", "x", "slab"))
    placed = (P(TILE, None, "slab"), P(TILE, None, "slab"), P(), P(TILE), P(TILE))
    return jax.shard_map(
        body, mesh=grid, in_specs=placed, out_specs=P(TILE, None, "slab"), check_vma=False
    )
```

time: 624 us -> 519 us (0.83)
  blocking collectives: 414 us -> 181 us
  local copies, waits for them, and re-layouts: 24.8 us -> 240 us
  waiting for transfers between devices: 128 us -> 0.04 us
  matrix products: 25.3 us -> 56 us
  other arithmetic: 8.23 us -> 18.3 us
    all_to_all x1 -> x2, blocking collectives: 414 us -> 53 us  [the longest x1 30.7 us: body(): lax.all_to_all(sums, PLANE + ('slab',), split_axis=0, concat_axis=0, tile...]
    all_gather x0 -> x1, blocking collectives: none -> 128 us  [body(): meta = lax.all_gather(jnp.stack([owner, res_ids]), PLANE)]
    all_to_all x1, waiting for transfers between devices: 115 us -> 0.01 us  [body(): got = lax.all_to_all(sent, PLANE, split_axis=0, concat_axis=0, tiled=True)]
    reshape x0 -> x19, local copies, waits for them, and re-layouts: none -> 93.6 us  [the longest x16 46.4 us: one(): picked = held[own_rows].reshape(tiles * part, wide)]
    gather x1 -> x16, local copies, waits for them, and re-layouts: 14.2 us -> 90.6 us  [one(): picked = held[own_rows].reshape(tiles * part, wide)]
    dot_general x3 -> x16, matrix products: 25.3 us -> 56 us  [one(): return jnp.dot(masked, picked, precision=lax.Precision.HIGHEST)]
    transpose x0 -> x1, local copies, waits for them, and re-layouts: none -> 21.4 us  [body(): integrals.reshape(tiles, rows, cell, part).transpose(2, 1, 0, 3)]
    broadcast_in_dim x0 -> x48, local copies, waits for them, and re-layouts: none -> 21 us  [the longest x32 19.7 us: one(): jnp.where(select[:, None, :], block_v[None], 0.0)]
  transfers between devices with their start and end apart: 2 -> 2, of which waited for: 2 -> 0; matrix products, arithmetic and copies ran while one was open for 0% -> 15% of each run, Pallas kernels for 0% -> 0%
where the time goes in v1:
time: 519 us; the launch traced here: 515 us
  local copies, waits for them, and re-layouts  240 us (46%)
  blocking collectives  181 us (35%)
  matrix products  56 us (11%)
  other arithmetic  18.3 us (4%)
  between operations  13.5 us (3%)
    all_gather x1, blocking collectives, body(): meta = lax.all_gather(jnp.stack([owner, res_ids]), PLANE)  128 us
    gather x16, local copies, waits for them, and re-layouts, one(): picked = held[own_rows].reshape(tiles * part, wide)  90.6 us
    dot_general x16, matrix products, one(): return jnp.dot(masked, picked, precision=lax.Precision.HIGHEST)  56 us
    reshape x16, local copies, waits for them, and re-layouts, one(): picked = held[own_rows].reshape(tiles * part, wide)  46.4 us
    reshape x2, local copies, waits for them, and re-layouts, body(): integrals.reshape(tiles, rows, cell, part).transpose(2, 1, 0, 3)  39.1 us
    all_to_all x1, blocking collectives, body(): lax.all_to_all(sums, PLANE + ('slab',), split_axis=0, concat_axis=0, tile...  30.7 us
    all_to_all x1, blocking collectives, body(): own = lax.all_to_all(own, PLANE, split_axis=0, concat_axis=0, tiled=True)  22.3 us
    transpose x1, local copies, waits for them, and re-layouts, body(): integrals.reshape(tiles, rows, cell, part).transpose(2, 1, 0, 3)  21.4 us
  transfers between devices with their start and end apart: 2, of which 0 were waited for; matrix products, arithmetic and copies ran while one was open for 15% of the time, Pallas kernels for 0%

profile of v1, /device:TPU:1, one launch (start us, length us, event | category | flops | bytes accessed | tf_op | source)
XLA Modules:
  0.0 514.6 jit_solution(18202100466202441607)
XLA Ops:
  7.8 22.3 %all_to_all.15 = f32[16,50,256]{2,1,0:T(8,128)S(1)} all-to-all(f32[16,50,256]{2,1,0:T(8,128)S(1)} %bitcast.58), channel_id=1, replica_groups=mesh['y'=4,'z'=8,'x'=4,'slab'=2] {'y','x'}, dimensions={0} | all-to-all | bytes 1638400 | tf_op jit(solution)/shard_map/all_to_all | solution.py:22
  31.3 21.0 %reshape.67 = f32[64,40,16,50]{3,2,1,0:T(8,128)} reshape(f32[64,40,800]{2,1,0:T(8,128)} %param.8) | data formatting | bytes 16384000 | tf_op jit(solution)/shard_map/reshape | solution.py:26
  52.3 21.4 %copy.17 = f32[16,40,64,50]{3,2,1,0:T(8,128)} copy(f32[16,40,64,50]{3,0,1,2:T(8,128)} %bitcast.55) | data formatting | bytes 16384000 | tf_op jit(solution)/shard_map/transpose | solution.py:26
  73.8 18.1 %reshape.68 = f32[16,40,3200]{2,1,0:T(8,128)} reshape(f32[16,40,64,50]{3,2,1,0:T(8,128)} %copy.17) | data formatting | bytes 16384000 | tf_op jit(solution)/shard_map/reshape | solution.py:26
  91.8 4.9 all-to-all-start
  97.0 127.9 %all-gather.2 = s32[16,2,64]{2,1,0:T(2,128)S(1)} all-gather(s32[1,2,64]{2,1,0:T(2,128)S(1)} %add_bitcast_fusion), channel_id=2, replica_groups=mesh['y'=4,'z'=8,'x'=4,'slab'=2] {'y','x'}, dimensions={0}, use_global_device_ids=true | all-gather | bytes 8704 | tf_op jit(solution)/shard_map/all_gather | solution.py:19
  225.0 8.1 %reshape.69 = f32[8,4,4,50,256]{4,2,1,0,3:T(4,128)} reshape(f32[128,50,256]{2,0,1:T(8,128)} %all-gather.5.cloned.1.call-done) | data formatting | bytes 13107200 | tf_op jit(solution)/shard_map/reshape | solution.py:24
  233.1 9.7 %copy.21 = f32[4,8,4,50,256]{4,3,2,1,0:T(8,128)} copy(f32[4,8,4,50,256]{4,2,0,1,3:T(4,128)} %bitcast.56) | data formatting | bytes 13107200 | tf_op jit(solution)/shard_map/while | solution.py:36
  242.8 232.0 %while.10 = (s32[]{:T(128)}, f32[16,80,256]{2,1,0:T(8,128)}, s32[16,64]{1,0:T(8,128)S(1)}, f32[16,40,3200]{2,1,0:T(8,128)}, s32[16,64]{1,0:T(8,128)S(1)}, /*index=5*/f32[128,50,256]{2,1,0:T(8,128)}, s32[]{:T(128)}) while((s32[]{:T(128)}, f32[16,80,256]{2,1,0:T(8,128)}, s32[16,64]{1,0:T(8,128)S(1)}, f32[16,40,3200]{2,1,0:T(8,128)}, ...), condition=%wide.region_2.3_spmd, body=%wide.region_1.2_spmd.sunk | while | flops 786689344 | bytes 20082264 | solution.py:36
  245.2 5.7 %gather_fusion = f32[64,50,256]{2,1,0:T(8,128)} fusion(f32[128,50,256]{2,1,0:T(8,128)} %get-tuple-element.128, s32[1024]{0:T(1024)S(1)} %pad_clamp_fusion.2), kind=kCustom, calls=%fused_computation.clone.1 | custom fusion | bytes 6553856 | tf_op jit(solution)/shard_map/while/body/eval_jaxpr/gather | solution.py:30
  253.8 3.5 fusion.17
  259.8 5.7 %gather_fusion = f32[64,50,256]{2,1,0:T(8,128)} fusion(f32[128,50,256]{2,1,0:T(8,128)} %get-tuple-element.128, s32[1024]{0:T(1024)S(1)} %pad_clamp_fusion.2), kind=kCustom, calls=%fused_computation.clone.1 | custom fusion | bytes 6553856 | tf_op jit(solution)/shard_map/while/body/eval_jaxpr/gather | solution.py:30
  268.3 3.5 fusion.17
  274.2 5.7 %gather_fusion = f32[64,50,256]{2,1,0:T(8,128)} fusion(f32[128,50,256]{2,1,0:T(8,128)} %get-tuple-element.128, s32[1024]{0:T(1024)S(1)} %pad_clamp_fusion.2), kind=kCustom, calls=%fused_computation.clone.1 | custom fusion | bytes 6553856 | tf_op jit(solution)/shard_map/while/body/eval_jaxpr/gather | solution.py:30
  279.9 2.9 reshape.92
  282.8 3.5 fusion.17
  288.8 5.7 %gather_fusion = f32[64,50,256]{2,1,0:T(8,128)} fusion(f32[128,50,256]{2,1,0:T(8,128)} %get-tuple-element.128, s32[1024]{0:T(1024)S(1)} %pad_clamp_fusion.2), kind=kCustom, calls=%fused_computation.clone.1 | custom fusion | bytes 6553856 | tf_op jit(solution)/shard_map/while/body/eval_jaxpr/gather | solution.py:30
  294.4 2.9 reshape.92
  297.3 3.5 fusion.17
  303.3 5.7 %gather_fusion = f32[64,50,256]{2,1,0:T(8,128)} fusion(f32[128,50,256]{2,1,0:T(8,128)} %get-tuple-element.128, s32[1024]{0:T(1024)S(1)} %pad_clamp_fusion.2), kind=kCustom, calls=%fused_computation.clone.1 | custom fusion | bytes 6553856 | tf_op jit(solution)/shard_map/while/body/eval_jaxpr/gather | solution.py:30
  308.9 2.9 reshape.92
  311.8 3.5 fusion.17
  317.8 5.7 %gather_fusion = f32[64,50,256]{2,1,0:T(8,128)} fusion(f32[128,50,256]{2,1,0:T(8,128)} %get-tuple-element.128, s32[1024]{0:T(1024)S(1)} %pad_clamp_fusion.2), kind=kCustom, calls=%fused_computation.clone.1 | custom fusion | bytes 6553856 | tf_op jit(solution)/shard_map/while/body/eval_jaxpr/gather | solution.py:30
  326.3 3.5 fusion.17
  332.3 5.7 %gather_fusion = f32[64,50,256]{2,1,0:T(8,128)} fusion(f32[128,50,256]{2,1,0:T(8,128)} %get-tuple-element.128, s32[1024]{0:T(1024)S(1)} %pad_clamp_fusion.2), kind=kCustom, calls=%fused_computation.clone.1 | custom fusion | bytes 6553856 | tf_op jit(solution)/shard_map/while/body/eval_jaxpr/gather | solution.py:30
  340.8 3.5 fusion.17
  346.8 5.7 %gather_fusion = f32[64,50,256]{2,1,0:T(8,128)} fusion(f32[128,50,256]{2,1,0:T(8,128)} %get-tuple-element.128, s32[1024]{0:T(1024)S(1)} %pad_clamp_fusion.2), kind=kCustom, calls=%fused_computation.clone.1 | custom fusion | bytes 6553856 | tf_op jit(solution)/shard_map/while/body/eval_jaxpr/gather | solution.py:30
  352.5 2.9 reshape.92
  355.4 3.5 fusion.17
  361.3 5.7 %gather_fusion = f32[64,50,256]{2,1,0:T(8,128)} fusion(f32[128,50,256]{2,1,0:T(8,128)} %get-tuple-element.128, s32[1024]{0:T(1024)S(1)} %pad_clamp_fusion.2), kind=kCustom, calls=%fused_computation.clone.1 | custom fusion | bytes 6553856 | tf_op jit(solution)/shard_map/while/body/eval_jaxpr/gather | solution.py:30
  367.0 2.9 reshape.92
  369.9 3.5 fusion.17
  375.8 5.7 %gather_fusion = f32[64,50,256]{2,1,0:T(8,128)} fusion(f32[128,50,256]{2,1,0:T(8,128)} %get-tuple-element.128, s32[1024]{0:T(1024)S(1)} %pad_clamp_fusion.2), kind=kCustom, calls=%fused_computation.clone.1 | custom fusion | bytes 6553856 | tf_op jit(solution)/shard_map/while/body/eval_jaxpr/gather | solution.py:30
  384.4 3.5 fusion.17
  390.3 5.7 %gather_fusion = f32[64,50,256]{2,1,0:T(8,128)} fusion(f32[128,50,256]{2,1,0:T(8,128)} %get-tuple-element.128, s32[1024]{0:T(1024)S(1)} %pad_clamp_fusion.2), kind=kCustom, calls=%fused_computation.clone.1 | custom fusion | bytes 6553856 | tf_op jit(solution)/shard_map/while/body/eval_jaxpr/gather | solution.py:30
  398.9 3.5 fusion.17
  404.8 5.7 %gather_fusion = f32[64,50,256]{2,1,0:T(8,128)} fusion(f32[128,50,256]{2,1,0:T(8,128)} %get-tuple-element.128, s32[1024]{0:T(1024)S(1)} %pad_clamp_fusion.2), kind=kCustom, calls=%fused_computation.clone.1 | custom fusion | bytes 6553856 | tf_op jit(solution)/shard_map/while/body/eval_jaxpr/gather | solution.py:30
  410.4 2.9 reshape.92
  413.4 3.5 fusion.17
  419.3 5.7 %gather_fusion = f32[64,50,256]{2,1,0:T(8,128)} fusion(f32[128,50,256]{2,1,0:T(8,128)} %get-tuple-element.128, s32[1024]{0:T(1024)S(1)} %pad_clamp_fusion.2), kind=kCustom, calls=%fused_computation.clone.1 | custom fusion | bytes 6553856 | tf_op jit(solution)/shard_map/while/body/eval_jaxpr/gather | solution.py:30
  427.9 3.5 fusion.17
  433.8 5.7 %gather_fusion = f32[64,50,256]{2,1,0:T(8,128)} fusion(f32[128,50,256]{2,1,0:T(8,128)} %get-tuple-element.128, s32[1024]{0:T(1024)S(1)} %pad_clamp_fusion.2), kind=kCustom, calls=%fused_computation.clone.1 | custom fusion | bytes 6553856 | tf_op jit(solution)/shard_map/while/body/eval_jaxpr/gather | solution.py:30
  442.4 3.5 fusion.17
  448.3 5.7 %gather_fusion = f32[64,50,256]{2,1,0:T(8,128)} fusion(f32[128,50,256]{2,1,0:T(8,128)} %get-tuple-element.128, s32[1024]{0:T(1024)S(1)} %pad_clamp_fusion.2), kind=kCustom, calls=%fused_computation.clone.1 | custom fusion | bytes 6553856 | tf_op jit(solution)/shard_map/while/body/eval_jaxpr/gather | solution.py:30
  456.9 3.5 fusion.17
  462.8 5.7 %gather_fusion = f32[64,50,256]{2,1,0:T(8,128)} fusion(f32[128,50,256]{2,1,0:T(8,128)} %get-tuple-element.128, s32[1024]{0:T(1024)S(1)} %pad_clamp_fusion.2), kind=kCustom, calls=%fused_computation.clone.1 | custom fusion | bytes 6553856 | tf_op jit(solution)/shard_map/while/body/eval_jaxpr/gather | solution.py:30
  471.4 3.5 fusion.17
  476.4 30.7 %all_to_all.16 = f32[32,80,128]{2,1,0:T(8,128)S(1)} all-to-all(f32[32,80,128]{2,1,0:T(8,128)S(1)} %bitcast.57), channel_id=1, replica_groups=mesh['y'=4,'z'=8,'x'=4,'slab'=2] {'y','x','slab'}, dimensions={0} | all-to-all | bytes 2621440 | tf_op jit(solution)/shard_map/all_to_all | solution.py:40
  (157 shorter events, 72.3 us)
Async XLA Ops:
  6.5 218.4 %all-gather.5.cloned.1.call-start = ((), (), s32[]{:S(2)}) async-start(), calls=%async_computation.3 | async-start | bytes 7372800 | tf_op jit(solution)/shard_map/all_gather | solution.py:23
  91.8 4.9 copy-start.1
  91.8 4.9 copy-start.2
  91.8 5.1 copy-start
  91.8 151.0 %all-to-all-start = ((f32[16,40,3200]{2,1,0:T(8,128)}), f32[16,40,3200]{2,1,0:T(8,128)}, u32[]{:S(2)}, u32[]{:S(2)}) async-start(f32[16,40,3200]{2,1,0:T(8,128)} %reshape.68), calls=%async_computation | async-start | bytes 16384000 | tf_op jit(solution)/shard_map/all_to_all | solution.py:27
Sparse Core Ops, SparseCore 0:
  31.4 77.0 all-gather.4

commit v2 on v1

v2 whole, which is shorter than its diff:
```python
import functools

import jax
import jax.numpy as jnp
from jax import lax
from jax.experimental import pallas as pl
from jax.experimental.pallas import tpu as pltpu
from jax.sharding import Mesh, PartitionSpec as P

RD = 2
PLANE = ("y", "x")
TILE = ("y", "z", "x")
LANES = 128
PITCH = 64
CHUNKS = ((0, 32), (32, 8))
VMEM = 56 * 1024 * 1024


def lane_ids():
    return lax.broadcasted_iota(jnp.int32, (8, LANES), 1)


def cut_kernel(part, v_ref, out_ref):
    tiles, _, depth = v_ref.shape
    cells = out_ref.shape[0]
    lane = lane_ids()
    full = depth // LANES

    def source(h, q):
        if q < full:
            return v_ref[h, :, q * LANES : (q + 1) * LANES]
        rest = v_ref[h, :, full * LANES : depth]
        return jnp.concatenate([rest, jnp.zeros((8, LANES - rest.shape[1]), rest.dtype)], axis=1)

    for c in range(cells):
        rolled = {}
        for j in range(tiles * part // LANES):
            made = None
            at = j * LANES
            while at < (j + 1) * LANES:
                h, v = divmod(at, part)
                q, o = divmod(c * part + v, LANES)
                run = min(part - v, LANES - o, (j + 1) * LANES - at)
                key = (h, q)
                if key not in rolled:
                    shift = (part * (h - c)) % LANES
                    rolled[key] = pltpu.roll(source(h, q), shift, 1) if shift else source(h, q)
                made = rolled[key] if made is None else jnp.where(lane >= at - j * LANES, rolled[key], made)
                at += run
            out_ref[c, :, j * LANES : (j + 1) * LANES] = made


def cut(integrals, cells, start, rows):
    tiles, _, depth = integrals.shape
    part = depth // cells
    return pl.pallas_call(
        functools.partial(cut_kernel, part),
        grid=(rows // 8,),
        in_specs=[pl.BlockSpec((tiles, 8, depth), lambda i: (0, i + start // 8, 0))],
        out_specs=pl.BlockSpec((cells, 8, tiles * part), lambda i: (0, i, 0)),
        out_shape=jax.ShapeDtypeStruct((cells, rows, tiles * part), jnp.float32),
        compiler_params=pltpu.CompilerParams(vmem_limit_bytes=VMEM),
        cost_estimate=pl.CostEstimate(flops=0, bytes_accessed=tiles * rows * depth * 8, transcendentals=0),
    )(integrals)


def split_kernel(part, t_ref, high_ref, low_ref):
    row = lax.broadcasted_iota(jnp.int32, (56, t_ref.shape[2]), 0)
    for s in range(t_ref.shape[0]):
        value = jnp.where(row < part, t_ref[s], 0.0)
        value = jnp.concatenate([value, jnp.zeros((PITCH - 56, value.shape[1]), value.dtype)], axis=0)
        high = value.astype(jnp.bfloat16)
        high_ref[s] = high
        low_ref[s] = (value - high.astype(jnp.float32)).astype(jnp.bfloat16)


def split(held, part):
    peers, rows, wide = held.shape
    block = 16
    shape = jax.ShapeDtypeStruct((peers, PITCH, wide), jnp.bfloat16)
    return pl.pallas_call(
        functools.partial(split_kernel, part),
        grid=(peers // block,),
        in_specs=[pl.BlockSpec((block, rows, wide), lambda i: (i, 0, 0))],
        out_specs=[pl.BlockSpec((block, PITCH, wide), lambda i: (i, 0, 0))] * 2,
        out_shape=(shape, shape),
        compiler_params=pltpu.CompilerParams(vmem_limit_bytes=VMEM),
        cost_estimate=pl.CostEstimate(flops=0, bytes_accessed=peers * wide * 480, transcendentals=0),
    )(held)


def ladder_kernel(part, own_ref, v_ref, mask_ref, high_ref, low_ref, out_ref):
    d = pl.program_id(0)
    rows = v_ref.shape[1]
    lane = lax.broadcasted_iota(jnp.int32, (rows, LANES), 1)
    total = jnp.zeros((2 * rows, high_ref.shape[2]), jnp.float32)

    def piece(h):
        q, o = divmod(part * h, LANES)
        base = PITCH * (h % 2)
        shift = (base - o) % LANES
        first = v_ref[0, :, q * LANES : (q + 1) * LANES]
        first = pltpu.roll(first, shift, 1) if shift else first
        if o + part <= LANES:
            return first
        second = v_ref[0, :, (q + 1) * LANES : (q + 2) * LANES]
        second = pltpu.roll(second, shift, 1) if shift else second
        return jnp.where(lane < base + LANES - o, first, second)

    for j in range(mask_ref.shape[1]):
        halves = []
        for k in range(2):
            h = 4 * j + 2 * k
            halves.append(jnp.where(lane < PITCH, piece(h), piece(h + 1)))
        value = jnp.concatenate(halves, axis=1)
        zeroth = value * mask_ref[0, j : j + 1, :]
        value = jnp.concatenate([zeroth, value - zeroth], axis=0)
        high = value.astype(jnp.bfloat16)
        low = (value - high.astype(jnp.float32)).astype(jnp.bfloat16)
        at = [own_ref[d, 4 * j + i] for i in range(4)]
        t_high = jnp.concatenate([high_ref[s] for s in at], axis=0)
        t_low = jnp.concatenate([low_ref[s] for s in at], axis=0)
        total += jnp.dot(high, t_high, preferred_element_type=jnp.float32)
        total += jnp.dot(low, t_high, preferred_element_type=jnp.float32)
        total += jnp.dot(high, t_low, preferred_element_type=jnp.float32)
    out_ref[0] = total[:, :LANES]
    out_ref[1] = total[:, LANES:]


def ladder(owners, got, masks, high, low, part):
    cell, rows, width = got.shape
    peers, _, wide = high.shape
    cores = wide // LANES
    groups = masks.shape[1]
    whole = pl.BlockSpec((peers, PITCH, wide), lambda d, own: (0, 0, 0), pipeline_mode=pl.Buffered(1))
    return pl.pallas_call(
        functools.partial(ladder_kernel, part),
        grid_spec=pltpu.PrefetchScalarGridSpec(
            num_scalar_prefetch=1,
            grid=(cell,),
            in_specs=[
                pl.BlockSpec((1, rows, width), lambda d, own: (d, 0, 0)),
                pl.BlockSpec((1, groups, 4 * PITCH), lambda d, own: (d, 0, 0)),
                whole,
                whole,
            ],
            out_specs=pl.BlockSpec((cores, RD * rows, LANES), lambda d, own: (d, 0, 0)),
        ),
        out_shape=jax.ShapeDtypeStruct((cell * cores, RD * rows, LANES), jnp.float32),
        compiler_params=pltpu.CompilerParams(vmem_limit_bytes=VMEM),
        cost_estimate=pl.CostEstimate(
            flops=6 * 2 * rows * cell * groups * 4 * PITCH * wide, bytes_accessed=4 * got.size + 4 * high.size, transcendentals=0
        ),
    )(owners, got, masks, high, low)


def exchange(value, axes):
    return lax.all_to_all(value, axes, split_axis=0, concat_axis=0, tiled=True)


def body(amplitudes, integrals, tile_map, cd_ids, res_ids):
    cell = lax.axis_size(PLANE)
    tiles, rows, depth = integrals.shape
    wide = amplitudes.shape[1]
    part = depth // cell
    peers = tile_map.shape[0]
    across, along = lax.axis_size("x"), lax.axis_size("z")
    positions = jnp.arange(peers, dtype=jnp.int32)
    at_x, at_z, at_y = positions % across, positions // across % along, positions // (across * along)
    slots = (at_z * lax.axis_size("y") + at_y) * across + at_x
    owner = jnp.sum(jnp.where(tile_map[None, :] == cd_ids[:, None], slots[None, :], 0), axis=1)
    ids = jnp.concatenate([owner, res_ids]).astype(jnp.float32)
    tail = jnp.zeros((56 - part, wide), jnp.float32).at[0, : 2 * tiles].set(ids)
    own = amplitudes[0].T.reshape(cell, part, wide)
    own = jnp.concatenate([own, jnp.broadcast_to(tail[None], (cell,) + tail.shape)], axis=1)
    own = exchange(own, PLANE)
    meta = own[:, part, : 2 * tiles].astype(jnp.int32)
    owners, targets = meta[:, :tiles], meta[:, tiles:]
    masks = jnp.repeat((targets == 0).astype(jnp.float32), PITCH, axis=1).reshape(cell, tiles // 4, 4 * PITCH)
    held = lax.all_gather(own, "z").reshape(peers, 56, wide)
    high, low = split(held, part)
    parts = []
    for start, count in CHUNKS:
        got = exchange(cut(integrals, cell, start, count), PLANE)
        sums = ladder(owners, got, masks, high, low, part)
        back = exchange(sums, PLANE + ("slab",))
        parts.append(jnp.sum(back, axis=0).reshape(RD, count, LANES))
    return jnp.concatenate(parts, axis=1)


def solution(mesh):
    grid = Mesh(mesh.devices.reshape(4, 8, 4, 2), ("y", "z", "x", "slab"))
    placed = (P(TILE, None, "slab"), P(TILE, None, "slab"), P(), P(TILE), P(TILE))
    return jax.shard_map(
        body, mesh=grid, in_specs=placed, out_specs=P(TILE, None, "slab"), check_vma=False
    )
```

time: 519 us -> 228 us (0.44)
  local copies, waits for them, and re-layouts: 240 us -> 4.45 us
  blocking collectives: 181 us -> 22.4 us
  waiting for transfers between devices: 0.04 us -> 91.3 us
  Pallas kernels: 0 us -> 67.3 us
  matrix products: 56 us -> 0 us
  starting transfers between devices: 4.88 us -> 25.5 us
  other arithmetic: 18.3 us -> 2.48 us
    all_gather x1 -> x0, blocking collectives: 128 us -> none  [body(): meta = lax.all_gather(jnp.stack([owner, res_ids]), PLANE)]
    reshape x19 -> x1, local copies, waits for them, and re-layouts: 93.6 us -> 1.24 us  [body(): own = amplitudes[0].T.reshape(cell, part, wide)]
    gather x16 -> x0, local copies, waits for them, and re-layouts: 90.6 us -> none  [one(): picked = held[own_rows].reshape(tiles * part, wide)]
    pallas_call x0 -> x5, Pallas kernels: none -> 67.3 us  [the longest x2 44.8 us: ladder(): pl.pallas_call(functools.partial(ladder_kernel, part), grid_spec=pltpu.Pr...]
    dot_general x16 -> x0, matrix products: 56 us -> none  [one(): return jnp.dot(masked, picked, precision=lax.Precision.HIGHEST)]
    all_to_all x1 -> x4, waiting for transfers between devices: 0.01 us -> 45.7 us  [exchange(): return lax.all_to_all(value, axes, split_axis=0, concat_axis=0, tiled=True)]
    all_gather x1, waiting for transfers between devices: 0.02 us -> 45.6 us  [body(): held = lax.all_gather(own, 'z').reshape(peers, 56, wide)]
    all_to_all x2 -> x1, blocking collectives: 53 us -> 22.4 us  [exchange(): return lax.all_to_all(value, axes, split_axis=0, concat_axis=0, tiled=True)]
  transfers between devices with their start and end apart: 2 -> 5, of which waited for: 0 -> 4; matrix products, arithmetic and copies ran while one was open for 15% -> 1% of each run, Pallas kernels for 0% -> 30%
where the time goes in v2:
time: 228 us; the launch traced here: 227 us
  waiting for transfers between devices  91.3 us (40%)
  Pallas kernels  67.3 us (30%)
  starting transfers between devices  25.5 us (11%)
  blocking collectives  22.4 us (10%)
  between operations  13.5 us (6%)
  local copies, waits for them, and re-layouts  4.45 us (2%)
  other arithmetic  2.48 us (1%)
    all_to_all x4, waiting for transfers between devices, exchange(): return lax.all_to_all(value, axes, split_axis=0, concat_axis=0, tiled=True)  45.7 us
    all_gather x1, waiting for transfers between devices, body(): held = lax.all_gather(own, 'z').reshape(peers, 56, wide)  45.6 us
    pallas_call x2, Pallas kernels, ladder(): pl.pallas_call(functools.partial(ladder_kernel, part), grid_spec=pltpu.Pr...  44.8 us
    all_to_all x4, starting transfers between devices, exchange(): return lax.all_to_all(value, axes, split_axis=0, concat_axis=0, tiled=True)  25.5 us
    all_to_all x1, blocking collectives, exchange(): return lax.all_to_all(value, axes, split_axis=0, concat_axis=0, tiled=True)  22.4 us
    pallas_call x2, Pallas kernels, cut(): pl.pallas_call(functools.partial(cut_kernel, part), grid=(rows // 8,), in...  13.8 us
    pallas_call x1, Pallas kernels, split(): pl.pallas_call(functools.partial(split_kernel, part), grid=(peers // bloc...  8.76 us
  transfers between devices with their start and end apart: 5, of which 4 were waited for; matrix products, arithmetic and copies ran while one was open for 1% of the time, Pallas kernels for 30%

profile of v2, /device:TPU:1, one launch (start us, length us, event | category | flops | bytes accessed | tf_op | source)
XLA Modules:
  0.0 226.9 jit_solution(10689089305545806803)
XLA Ops:
  6.5 0.0 all-gather.3.cloned.1.call-start
  6.5 1.2 reshape.112
  7.8 0.8 select_reduce_fusion
  8.6 0.7 add_convert_fusion
  9.4 0.1 pad_maximum_fusion
  9.5 22.4 %all_to_all.25 = f32[16,56,256]{2,1,0:T(8,128)} all-to-all(f32[16,56,256]{2,1,0:T(8,128)S(1)} %pad_maximum_fusion), channel_id=1, replica_groups=mesh['y'=4,'z'=8,'x'=4,'slab'=2] {'y','x'}, dimensions={0} | all-to-all | bytes 1835008 | tf_op jit(solution)/shard_map/all_to_all | solution.py:158
  31.8 0.0 all-gather.3.cloned.1.call-update
  31.9 4.2 %shard_map.58 = f32[16,8,3200]{2,1,0:T(8,128)} custom-call(f32[64,40,800]{2,1,0:T(8,128)} %v_ref.3), custom_call_target="tpu_custom_call" | custom-call | bytes 3276800 | tf_op jit(solution)/shard_map/pallas_call | solution.py:56
  36.1 3.7 %all-to-all-start.3 = ((f32[16,8,3200]{2,1,0:T(8,128)}), f32[16,8,3200]{2,1,0:T(8,128)S(1)}, u32[]{:S(2)}, u32[]{:S(2)}) async-start(f32[16,8,3200]{2,1,0:T(8,128)} %shard_map.58), calls=%async_computation.3 | async-start | bytes 3276800 | tf_op jit(solution)/shard_map/all_to_all | solution.py:158
  39.8 9.6 %shard_map.55 = f32[16,32,3200]{2,1,0:T(8,128)} custom-call(f32[64,40,800]{2,1,0:T(8,128)} %v_ref.3), custom_call_target="tpu_custom_call" | custom-call | bytes 13107200 | tf_op jit(solution)/shard_map/pallas_call | solution.py:56
  49.4 11.8 %all-to-all-done.3.v_ref = f32[16,8,3200]{2,1,0:T(8,128)S(1)} async-done(((f32[16,8,3200]{2,1,0:T(8,128)}), f32[16,8,3200]{2,1,0:T(8,128)S(1)}, u32[]{:S(2)}, u32[]{:S(2)}) %all-to-all-start.3) | async-done | bytes 1638432 | tf_op jit(solution)/shard_map/all_to_all | solution.py:158
  61.2 0.0 copy-start
  61.2 1.2 copy-done
  62.4 6.4 %all-to-all-start.1 = ((f32[16,32,3200]{2,1,0:T(8,128)}), f32[16,32,3200]{2,1,0:T(8,128)}, u32[]{:S(2)}, u32[]{:S(2)}) async-start(f32[16,32,3200]{2,1,0:T(8,128)} %shard_map.55), calls=%async_computation.1 | async-start | bytes 13107200 | tf_op jit(solution)/shard_map/all_to_all | solution.py:158
  68.9 0.8 slice.28
  69.7 0.0 copy-start.1
  69.7 0.1 fusion
  69.8 0.2 broadcast_in_dim.28
  70.0 0.9 reshape_reshape.3.mask_ref
  70.9 45.6 %all-gather.3.cloned.1.call-done.t_ref = f32[128,56,256]{2,1,0:T(8,128)} async-done(((f32[16,56,256]{2,1,0:T(8,128)}), f32[128,56,256]{2,1,0:T(8,128)}) %all-gather.3.cloned.1.call-update) | async-done | bytes 7340048 | tf_op jit(solution)/shard_map/all_gather | solution.py:180
  116.5 8.8 %shard_map.56 = (bf16[128,64,256]{2,1,0:T(8,128)(2,1)}, bf16[128,64,256]{2,1,0:T(8,128)(2,1)}) custom-call(f32[128,56,256]{2,1,0:T(8,128)} %all-gather.3.cloned.1.call-done.t_ref), custom_call_target="tpu_custom_call" | custom-call | bytes 15728640 | tf_op jit(solution)/shard_map/pallas_call | solution.py:81
  125.3 0.0 copy-done.1
  125.3 20.8 %shard_map.59 = f32[32,16,128]{2,1,0:T(8,128)} custom-call(s32[16,64]{1,0:T(8,128)} %bitcast.13, f32[16,8,3200]{2,1,0:T(8,128)} %copy-done, f32[16,16,256]{2,1,0:T(8,128)} %reshape_reshape.3.mask_ref, bf16[128,64,256]{2,1,0:T(8,128)(2,1)} %get-tuple-element.19.high_ref, bf16[128,64,256]{2,1,0:T(8,128)(2,1)} %get-tuple-element.20.low_ref), custom_call_target="tpu_custom_call" | custom-call | flops 1610612736 | bytes 10027008 | tf_op jit(solution)/shard_map/pallas_call | solution.py:136
  146.1 16.7 %all-to-all-done.1.v_ref = f32[16,32,3200]{2,1,0:T(8,128)} async-done(((f32[16,32,3200]{2,1,0:T(8,128)}), f32[16,32,3200]{2,1,0:T(8,128)}, u32[]{:S(2)}, u32[]{:S(2)}) %all-to-all-start.1) | async-done | bytes 6553632 | tf_op jit(solution)/shard_map/all_to_all | solution.py:158
  162.8 8.0 %all-to-all-start.4 = ((f32[32,16,128]{2,1,0:T(8,128)}), f32[32,16,128]{2,1,0:T(8,128)S(1)}, u32[]{:S(2)}, u32[]{:S(2)}) async-start(f32[32,16,128]{2,1,0:T(8,128)} %shard_map.59), calls=%async_computation.4 | async-start | bytes 524288 | tf_op jit(solution)/shard_map/all_to_all | solution.py:158
  170.8 24.0 %shard_map.57 = f32[32,64,128]{2,1,0:T(8,128)} custom-call(s32[16,64]{1,0:T(8,128)} %bitcast.14, f32[16,32,3200]{2,1,0:T(8,128)} %all-to-all-done.1.v_ref, f32[16,16,256]{2,1,0:T(8,128)} %reshape_reshape.3.mask_ref, bf16[128,64,256]{2,1,0:T(8,128)(2,1)} %get-tuple-element.19.high_ref, bf16[128,64,256]{2,1,0:T(8,128)(2,1)} %get-tuple-element.20.low_ref), custom_call_target="tpu_custom_call" | custom-call | flops 6442450944 | bytes 14942208 | tf_op jit(solution)/shard_map/pallas_call | solution.py:136
  194.8 0.0 all-to-all-done.4
  194.8 7.4 %all-to-all-start.2 = ((f32[32,64,128]{2,1,0:T(8,128)}), f32[32,64,128]{2,1,0:T(8,128)S(1)}, u32[]{:S(2)}, u32[]{:S(2)}) async-start(f32[32,64,128]{2,1,0:T(8,128)} %shard_map.57), calls=%async_computation.2 | async-start | bytes 2097152 | tf_op jit(solution)/shard_map/all_to_all | solution.py:158
  202.2 17.1 %all-to-all-done.2 = f32[32,64,128]{2,1,0:T(8,128)S(1)} async-done(((f32[32,64,128]{2,1,0:T(8,128)}), f32[32,64,128]{2,1,0:T(8,128)S(1)}, u32[]{:S(2)}, u32[]{:S(2)}) %all-to-all-start.2) | async-done | bytes 1048608 | tf_op jit(solution)/shard_map/all_to_all | solution.py:158
  219.3 0.1 reduce_sum.28
  219.4 0.6 pad_maximum_fusion.1
  (5 shorter events, 0.1 us)
Async XLA Ops:
  6.5 110.0 %all-gather.3.cloned.1.call-start = ((), (), s32[]{:S(2)}) async-start(), calls=%async_computation.5 | async-start | bytes 8257536 | tf_op jit(solution)/shard_map/all_gather | solution.py:180
  36.1 25.1 %all-to-all-start.3 = ((f32[16,8,3200]{2,1,0:T(8,128)}), f32[16,8,3200]{2,1,0:T(8,128)S(1)}, u32[]{:S(2)}, u32[]{:S(2)}) async-start(f32[16,8,3200]{2,1,0:T(8,128)} %shard_map.58), calls=%async_computation.3 | async-start | bytes 3276800 | tf_op jit(solution)/shard_map/all_to_all | solution.py:158
  61.2 1.2 copy-start
  62.4 100.4 %all-to-all-start.1 = ((f32[16,32,3200]{2,1,0:T(8,128)}), f32[16,32,3200]{2,1,0:T(8,128)}, u32[]{:S(2)}, u32[]{:S(2)}) async-start(f32[16,32,3200]{2,1,0:T(8,128)} %shard_map.55), calls=%async_computation.1 | async-start | bytes 13107200 | tf_op jit(solution)/shard_map/all_to_all | solution.py:158
  69.7 55.5 %copy-start.1 = (s32[16,128]{1,0:T(8,128)}, s32[16,128]{1,0:T(8,128)S(1)}, u32[]{:S(2)}) copy-start(s32[16,128]{1,0:T(8,128)S(1)} %convert_bitcast_fusion) | copy-start | bytes 24580
  162.8 32.0 %all-to-all-start.4 = ((f32[32,16,128]{2,1,0:T(8,128)}), f32[32,16,128]{2,1,0:T(8,128)S(1)}, u32[]{:S(2)}, u32[]{:S(2)}) async-start(f32[32,16,128]{2,1,0:T(8,128)} %shard_map.59), calls=%async_computation.4 | async-start | bytes 524288 | tf_op jit(solution)/shard_map/all_to_all | solution.py:158
  194.8 24.6 %all-to-all-start.2 = ((f32[32,64,128]{2,1,0:T(8,128)}), f32[32,64,128]{2,1,0:T(8,128)S(1)}, u32[]{:S(2)}, u32[]{:S(2)}) async-start(f32[32,64,128]{2,1,0:T(8,128)} %shard_map.57), calls=%async_computation.2 | async-start | bytes 2097152 | tf_op jit(solution)/shard_map/all_to_all | solution.py:158
Sparse Core Ops, SparseCore 0:
  32.0 84.4 all-gather.2

commit v3 on v2

v3 whole, which is shorter than its diff:
```python
import functools

import jax
import jax.numpy as jnp
from jax import lax
from jax.experimental import pallas as pl
from jax.experimental.pallas import tpu as pltpu
from jax.sharding import Mesh, PartitionSpec as P

RD = 2
PLANE = ("y", "x")
TILE = ("y", "z", "x")
LANES = 128
PITCH = 64
PADDED = 56
VMEM = 20 * 1024 * 1024


def pack_kernel(part, tiles, shape, map_ref, cd_ref, res_ref, t_ref, out_ref, order_ref):
    size_y, size_z, size_x = shape
    square = (LANES, LANES)
    lane = lax.broadcasted_iota(jnp.int32, square, 1)
    row = lax.broadcasted_iota(jnp.int32, square, 0)

    def down(values):
        return jnp.transpose(jnp.broadcast_to(values, square))

    def wide(ref):
        values = ref[...].astype(jnp.float32)
        return jnp.concatenate([values, jnp.zeros((1, LANES - values.shape[1]), jnp.float32)], axis=1)

    cd, target = wide(cd_ref), wide(res_ref)
    at_x, at_z, at_y = row % size_x, row // size_x % size_z, row // (size_x * size_z)
    slot = ((at_z * size_y + at_y) * size_x + at_x).astype(jnp.float32)
    match = down(map_ref[...].astype(jnp.float32)) == cd
    owner = jnp.sum(jnp.where(match, slot, 0.0), axis=0, keepdims=True)
    key = target * tiles + lane[:1].astype(jnp.float32)
    rank = jnp.sum(jnp.where((down(key) < key) & (row < tiles), 1.0, 0.0), axis=0, keepdims=True)
    here = (down(rank) == lane.astype(jnp.float32)) & (row < tiles)
    order = jnp.sum(jnp.where(here, row.astype(jnp.float32), 0.0), axis=0, keepdims=True)
    owner = jnp.sum(jnp.where(here, down(owner), 0.0), axis=0, keepdims=True)
    zeros = jnp.sum(jnp.where((lane[:1] < tiles) & (target == 0.0), 1.0, 0.0), axis=1, keepdims=True)
    order_ref[...] = order.astype(jnp.int32)
    ids = jnp.where(lane[:1] == tiles, zeros, owner)
    tail = jnp.zeros((PADDED - part, t_ref.shape[1]), jnp.float32)
    for c in range(out_ref.shape[0]):
        out_ref[c, :part, :] = t_ref[c * part : (c + 1) * part, :]
        out_ref[c, part:, :] = tail
        out_ref[c, part : part + 1, :LANES] = ids


def pack(tile_map, cd_ids, res_ids, turned, cell, shape):
    depth, wide = turned.shape
    part = depth // cell
    tiles = cd_ids.shape[0]
    return pl.pallas_call(
        functools.partial(pack_kernel, part, tiles, shape),
        out_shape=(
            jax.ShapeDtypeStruct((cell, PADDED, wide), jnp.float32),
            jax.ShapeDtypeStruct((1, LANES), jnp.int32),
        ),
        compiler_params=pltpu.CompilerParams(vmem_limit_bytes=VMEM),
        cost_estimate=pl.CostEstimate(flops=0, bytes_accessed=depth * wide * 8, transcendentals=0),
    )(tile_map[None], cd_ids[None], res_ids[None], turned)


def cut_kernel(part, order_ref, v_ref, out_ref):
    tiles, _, depth = v_ref.shape
    cells = out_ref.shape[0]
    lane = lax.broadcasted_iota(jnp.int32, (8, LANES), 1)
    full = depth // LANES
    order = [order_ref[0, h] for h in range(tiles)]

    def source(h, q):
        if q < full:
            return v_ref[order[h], :, q * LANES : (q + 1) * LANES]
        rest = v_ref[order[h], :, full * LANES : depth]
        return jnp.concatenate([rest, jnp.zeros((8, LANES - rest.shape[1]), rest.dtype)], axis=1)

    for c in range(cells):
        rolled = {}
        for j in range(tiles * part // LANES):
            made = None
            at = j * LANES
            while at < (j + 1) * LANES:
                h, v = divmod(at, part)
                q, o = divmod(c * part + v, LANES)
                run = min(part - v, LANES - o, (j + 1) * LANES - at)
                key = (h, q)
                if key not in rolled:
                    shift = (part * (h - c)) % LANES
                    rolled[key] = pltpu.roll(source(h, q), shift, 1) if shift else source(h, q)
                made = rolled[key] if made is None else jnp.where(lane >= at - j * LANES, rolled[key], made)
                at += run
            out_ref[c, :, j * LANES : (j + 1) * LANES] = made


def cut(order, integrals, cells):
    tiles, rows, depth = integrals.shape
    part = depth // cells
    return pl.pallas_call(
        functools.partial(cut_kernel, part),
        grid_spec=pltpu.PrefetchScalarGridSpec(
            num_scalar_prefetch=1,
            grid=(rows // 8,),
            in_specs=[pl.BlockSpec((tiles, 8, depth), lambda i, order: (0, i, 0))],
            out_specs=pl.BlockSpec((cells, 8, tiles * part), lambda i, order: (0, i, 0)),
        ),
        out_shape=jax.ShapeDtypeStruct((cells, rows, tiles * part), jnp.float32),
        compiler_params=pltpu.CompilerParams(vmem_limit_bytes=VMEM),
        cost_estimate=pl.CostEstimate(flops=0, bytes_accessed=tiles * rows * depth * 8, transcendentals=0),
    )(order, integrals)


def split_kernel(part, t_ref, high_ref, low_ref):
    row = lax.broadcasted_iota(jnp.int32, (PADDED, t_ref.shape[2]), 0)
    for s in range(t_ref.shape[0]):
        value = jnp.where(row < part, t_ref[s], 0.0)
        value = jnp.concatenate([value, jnp.zeros((PITCH - PADDED, value.shape[1]), value.dtype)], axis=0)
        high = value.astype(jnp.bfloat16)
        high_ref[s] = high
        low_ref[s] = (value - high.astype(jnp.float32)).astype(jnp.bfloat16)


def split(held, part):
    peers, rows, wide = held.shape
    block = 16
    shape = jax.ShapeDtypeStruct((peers, PITCH, wide), jnp.bfloat16)
    return pl.pallas_call(
        functools.partial(split_kernel, part),
        grid=(peers // block,),
        in_specs=[pl.BlockSpec((block, rows, wide), lambda i: (i, 0, 0))],
        out_specs=[pl.BlockSpec((block, PITCH, wide), lambda i: (i, 0, 0))] * 2,
        out_shape=(shape, shape),
        compiler_params=pltpu.CompilerParams(vmem_limit_bytes=VMEM),
        cost_estimate=pl.CostEstimate(flops=0, bytes_accessed=peers * wide * 480, transcendentals=0),
    )(held)


def ladder_kernel(part, meta_ref, v_ref, high_ref, low_ref, out_ref, kept_ref, major_ref, minor_ref):
    d = pl.program_id(0)
    rows = v_ref.shape[1]
    tiles = v_ref.shape[2] // part
    groups = tiles // 4
    lane = lax.broadcasted_iota(jnp.int32, (rows, LANES), 1)
    spread = lax.broadcasted_iota(jnp.int32, (rows, 4 * PITCH), 1)
    zeros = meta_ref[d, tiles]
    mixed = jnp.minimum(zeros // 4, groups - 1)
    edge = (zeros - 4 * mixed) * PITCH

    def piece(h):
        q, o = divmod(part * h, LANES)
        base = PITCH * (h % 2)
        shift = (base - o) % LANES
        first = v_ref[0, :, q * LANES : (q + 1) * LANES]
        first = pltpu.roll(first, shift, 1) if shift else first
        if o + part <= LANES:
            return first
        second = v_ref[0, :, (q + 1) * LANES : (q + 2) * LANES]
        second = pltpu.roll(second, shift, 1) if shift else second
        return jnp.where(lane < base + LANES - o, first, second)

    def add(value, j, target):
        rest = value - value.astype(jnp.bfloat16).astype(jnp.float32)
        both = jnp.concatenate([value, rest], axis=0).astype(jnp.bfloat16)
        at = [meta_ref[d, 4 * j + i] for i in range(4)]
        t_high = jnp.concatenate([high_ref[s] for s in at], axis=0)
        t_low = jnp.concatenate([low_ref[s] for s in at], axis=0)
        major_ref[target] += jnp.dot(both, t_high, preferred_element_type=jnp.float32)
        minor_ref[target] += jnp.dot(both[:rows], t_low, preferred_element_type=jnp.float32)

    major_ref[...] = jnp.zeros(major_ref.shape, jnp.float32)
    minor_ref[...] = jnp.zeros(minor_ref.shape, jnp.float32)
    for j in range(groups):
        halves = []
        for k in range(2):
            h = 4 * j + 2 * k
            halves.append(jnp.where(lane < PITCH, piece(h), piece(h + 1)))
        value = jnp.concatenate(halves, axis=1)
        kept_ref[j] = value
        start = jnp.where(mixed == j, edge, 0)
        add(jnp.where(spread >= start, value, 0.0), j, jnp.where(mixed <= j, 1, 0))
    add(jnp.where(spread < edge, kept_ref[mixed], 0.0), mixed, 0)
    for t in range(RD):
        total = major_ref[t, :rows] + major_ref[t, rows:] + minor_ref[t]
        for k in range(out_ref.shape[0]):
            out_ref[k, 0, t * rows : (t + 1) * rows, :] = total[:, k * LANES : (k + 1) * LANES]


def ladder(meta, got, high, low, part):
    cell, rows, width = got.shape
    peers, _, wide = high.shape
    cores = wide // LANES
    groups = width // part // 4
    whole = pl.BlockSpec((peers, PITCH, wide), lambda d, meta: (0, 0, 0), pipeline_mode=pl.Buffered(1))
    return pl.pallas_call(
        functools.partial(ladder_kernel, part),
        grid_spec=pltpu.PrefetchScalarGridSpec(
            num_scalar_prefetch=1,
            grid=(cell,),
            in_specs=[pl.BlockSpec((1, rows, width), lambda d, meta: (d, 0, 0)), whole, whole],
            out_specs=pl.BlockSpec((cores, 1, RD * rows, LANES), lambda d, meta: (0, d, 0, 0)),
            scratch_shapes=[
                pltpu.VMEM((groups, rows, 4 * PITCH), jnp.float32),
                pltpu.VMEM((RD, 2 * rows, wide), jnp.float32),
                pltpu.VMEM((RD, rows, wide), jnp.float32),
            ],
        ),
        out_shape=jax.ShapeDtypeStruct((cores, cell, RD * rows, LANES), jnp.float32),
        compiler_params=pltpu.CompilerParams(vmem_limit_bytes=VMEM),
        cost_estimate=pl.CostEstimate(
            flops=6 * rows * cell * groups * 4 * PITCH * wide, bytes_accessed=4 * got.size + 4 * high.size, transcendentals=0
        ),
    )(meta, got, high, low)


def exchange(value, axes):
    return lax.all_to_all(value, axes, split_axis=0, concat_axis=0, tiled=True)


def body(amplitudes, integrals, tile_map, cd_ids, res_ids):
    cell = lax.axis_size(PLANE)
    tiles, rows, depth = integrals.shape
    wide = amplitudes.shape[1]
    part = depth // cell
    peers = tile_map.shape[0]
    shape = tuple(lax.axis_size(a) for a in TILE)
    own, order = pack(tile_map, cd_ids, res_ids, amplitudes[0].T, cell, shape)
    own = exchange(own, PLANE)
    shared = lax.all_gather(own, "z")
    meta = own[:, part, :LANES].astype(jnp.int32)
    sent, meta = lax.optimization_barrier((cut(order, integrals, cell), meta))
    got = exchange(sent, PLANE)
    got, shared, meta = lax.optimization_barrier((got, shared, meta))
    high, low = split(shared.reshape(peers, PADDED, wide), part)
    sums = ladder(meta, got, high, low, part)
    core = lax.axis_index("slab")
    mine = lax.dynamic_index_in_dim(sums, core, 0, keepdims=False)
    other = lax.dynamic_index_in_dim(sums, 1 - core, 0, keepdims=False)
    mine += lax.ppermute(other, "slab", [(0, 1), (1, 0)])
    back = exchange(mine, PLANE)
    return jnp.sum(back, axis=0).reshape(RD, rows, LANES)


def solution(mesh):
    grid = Mesh(mesh.devices.reshape(4, 8, 4, 2), TILE + ("slab",))
    placed = (P(TILE, None, "slab"), P(TILE, None, "slab"), P(), P(TILE), P(TILE))
    return jax.shard_map(
        body, mesh=grid, in_specs=placed, out_specs=P(TILE, None, "slab"), check_vma=False
    )
```

time: 228 us -> 225 us (0.987)
  Pallas kernels: 67.3 us -> 28.5 us
  waiting for transfers between devices: 91.3 us -> 120 us
  starting transfers between devices: 25.5 us -> 7.53 us
  blocking collectives: 22.4 us -> 39.7 us
  local copies, waits for them, and re-layouts: 4.45 us -> 13.9 us
    all_to_all x4 -> x1, waiting for transfers between devices: 45.7 us -> 118 us  [exchange(): return lax.all_to_all(value, axes, split_axis=0, concat_axis=0, tiled=True)]
    all_gather x1, waiting for transfers between devices: 45.6 us -> 0.01 us  [body(): shared = lax.all_gather(own, 'z')]
    pallas_call x2 -> x1, Pallas kernels: 44.8 us -> 17.9 us  [ladder(): pl.pallas_call(functools.partial(ladder_kernel, part), grid_spec=pltpu.Pr...]
    all_to_all x4 -> x1, starting transfers between devices: 25.5 us -> 4.75 us  [exchange(): return lax.all_to_all(value, axes, split_axis=0, concat_axis=0, tiled=True)]
    all_to_all x1 -> x2, blocking collectives: 22.4 us -> 39.7 us  [exchange(): return lax.all_to_all(value, axes, split_axis=0, concat_axis=0, tiled=True)]
    unnamed x4 -> x14, local copies, waits for them, and re-layouts: 1.25 us -> 13 us
    pallas_call x1, Pallas kernels: 8.76 us -> 1.04 us  [split(): pl.pallas_call(functools.partial(split_kernel, part), grid=(peers // bloc...]
    pallas_call x2, Pallas kernels: 13.8 us -> 9.6 us  [the longest x1 9.4 us: cut(): pl.pallas_call(functools.partial(cut_kernel, part), grid_spec=pltpu.Prefe...]
  transfers between devices with their start and end apart: 5 -> 3, of which waited for: 4 -> 2; matrix products, arithmetic and copies ran while one was open for 1% -> 0% of each run, Pallas kernels for 30% -> 4%
where the time goes in v3:
time: 225 us; the launch traced here: 224 us
  waiting for transfers between devices  120 us (53%)
  blocking collectives  39.7 us (18%)
  Pallas kernels  28.5 us (13%)
  local copies, waits for them, and re-layouts  13.9 us (6%)
  between operations  13.5 us (6%)
  starting transfers between devices  7.53 us (3%)
    all_to_all x1, waiting for transfers between devices, exchange(): return lax.all_to_all(value, axes, split_axis=0, concat_axis=0, tiled=True)  118 us
    all_to_all x2, blocking collectives, exchange(): return lax.all_to_all(value, axes, split_axis=0, concat_axis=0, tiled=True)  39.7 us
    pallas_call x1, Pallas kernels, ladder(): pl.pallas_call(functools.partial(ladder_kernel, part), grid_spec=pltpu.Pr...  17.9 us
    unnamed x14, local copies, waits for them, and re-layouts  13 us
    pallas_call x1, Pallas kernels, cut(): pl.pallas_call(functools.partial(cut_kernel, part), grid_spec=pltpu.Prefe...  9.4 us
    all_to_all x1, starting transfers between devices, exchange(): return lax.all_to_all(value, axes, split_axis=0, concat_axis=0, tiled=True)  4.75 us
  transfers between devices with their start and end apart: 3, of which 2 were waited for; matrix products, arithmetic and copies ran while one was open for 0% of the time, Pallas kernels for 4%

profile of v3, /device:TPU:1, one launch (start us, length us, event | category | flops | bytes accessed | tf_op | source)
XLA Modules:
  0.0 224.0 jit_solution(5557535832992139668)
XLA Ops:
  6.5 0.0 all-gather.3.cloned.1.call-start
  6.5 0.0 copy-start.3
  6.5 1.1 copy-done.3
  7.7 0.0 copy-start.4
  7.7 0.7 copy-done.4
  8.3 0.0 copy-start.5
  8.3 0.7 copy-done.5
  9.0 0.0 copy-start.6
  9.0 0.7 copy-done.6
  9.7 0.2 shard_map.55
  9.9 22.4 %all_to_all.15 = f32[16,56,256]{2,1,0:T(8,128)} all-to-all(f32[16,56,256]{2,1,0:T(8,128)S(1)} %get-tuple-element.15), channel_id=1, replica_groups=mesh['y'=4,'z'=8,'x'=4,'slab'=2] {'y','x'}, dimensions={0} | all-to-all | bytes 1835008 | tf_op jit(solution)/shard_map/all_to_all | solution.py:218
  32.2 0.0 all-gather.3.cloned.1.call-update
  32.2 0.0 copy-start.1
  32.3 3.6 %copy-done.1 = f32[64,40,800]{2,1,0:T(8,128)S(1)} copy-done((f32[64,40,800]{2,1,0:T(8,128)S(1)}, f32[64,40,800]{2,1,0:T(8,128)}, u32[]{:S(2)}) %copy-start.1) | copy-done | bytes 8192024
  35.9 9.4 %shard_map.56 = f32[16,40,3200]{2,1,0:T(8,128)S(1)} custom-call(s32[1,128]{1,0:T(1,128)S(1)} %get-tuple-element.14.order_ref, f32[64,40,800]{2,1,0:T(8,128)S(1)} %copy-done.1), custom_call_target="tpu_custom_call" | custom-call | bytes 16384000 | tf_op jit(solution)/shard_map/pallas_call | solution.py:101
  45.3 0.0 copy-start
  45.3 3.2 %copy-done = f32[16,40,3200]{2,1,0:T(8,128)} copy-done((f32[16,40,3200]{2,1,0:T(8,128)}, f32[16,40,3200]{2,1,0:T(8,128)S(1)}, u32[]{:S(2)}) %copy-start) | copy-done | bytes 8192024
  48.4 0.8 slice.4
  49.3 4.7 %all-to-all-start.1 = ((f32[16,40,3200]{2,1,0:T(8,128)}), f32[16,40,3200]{2,1,0:T(8,128)}, u32[]{:S(2)}, u32[]{:S(2)}) async-start(f32[16,40,3200]{2,1,0:T(8,128)} %copy-done), calls=%async_computation.1 | async-start | bytes 16384000 | tf_op jit(solution)/shard_map/all_to_all | solution.py:218
  54.1 118.4 %all-to-all-done.1.v_ref = f32[16,40,3200]{2,1,0:T(8,128)} async-done(((f32[16,40,3200]{2,1,0:T(8,128)}), f32[16,40,3200]{2,1,0:T(8,128)}, u32[]{:S(2)}, u32[]{:S(2)}) %all-to-all-start.1) | async-done | bytes 8192032 | tf_op jit(solution)/shard_map/all_to_all | solution.py:218
  172.5 0.0 all-gather.3.cloned.1.call-done
  172.5 0.0 copy-start.2
  172.5 3.1 %copy-done.2 = f32[128,56,256]{2,1,0:T(8,128)S(1)} copy-done((f32[128,56,256]{2,1,0:T(8,128)S(1)}, f32[128,56,256]{2,1,0:T(8,128)}, u32[]{:S(2)}) %copy-start.2) | copy-done | bytes 7340056
  175.6 1.0 shard_map.57
  176.6 17.9 %shard_map.58 = f32[2,16,80,128]{3,2,1,0:T(8,128)S(1)} custom-call(s32[16,128]{1,0:T(8,128)S(1)} %convert_bitcast_fusion.meta_ref, f32[16,40,3200]{2,1,0:T(8,128)} %all-to-all-done.1.v_ref, bf16[128,64,256]{2,1,0:T(8,128)(2,1)S(1)} %get-tuple-element.21.high_ref, bf16[128,64,256]{2,1,0:T(8,128)(2,1)S(1)} %get-tuple-element.22.low_ref), custom_call_target="tpu_custom_call" | custom-call | flops 4026531840 | bytes 16580608 | tf_op jit(solution)/shard_map/pallas_call | solution.py:196
  194.5 0.1 dynamic-slice_bitcast_fusion
  194.5 2.8 %collective-permute-start = (f32[16,80,128]{2,1,0:T(8,128)S(1)}, f32[16,80,128]{2,1,0:T(8,128)S(1)}, u32[]{:S(2)}, u32[]{:S(2)}) collective-permute-start(f32[16,80,128]{2,1,0:T(8,128)S(1)} %dynamic-slice_bitcast_fusion), channel_id=1, source_target_pairs={{0,1},{1,0},{2,3},{3,2},{4,5},{5,4},{6,7},{7,6},{8,9},{9,8},{10,11... | collective-permute-start | bytes 1966088 | tf_op jit(solution)/shard_map/ppermute | solution.py:240
  197.3 1.7 collective-permute-done
  199.1 0.1 bitcast_add_fusion
  199.1 17.4 %all_to_all.16 = f32[16,80,128]{2,1,0:T(8,128)S(1)} all-to-all(f32[16,80,128]{2,1,0:T(8,128)S(1)} %bitcast_add_fusion), channel_id=1, replica_groups=mesh['y'=4,'z'=8,'x'=4,'slab'=2] {'y','x'}, dimensions={0} | all-to-all | bytes 1310720 | tf_op jit(solution)/shard_map/all_to_all | solution.py:218
  216.5 0.7 reduce_sum.9
  (1 shorter events, 0.0 us)
Async XLA Ops:
  6.5 165.9 %all-gather.3.cloned.1.call-start = ((), (), s32[]{:S(2)}) async-start(), calls=%async_computation.3 | async-start | bytes 8257536 | tf_op jit(solution)/shard_map/all_gather | solution.py:230
  6.5 1.1 copy-start.3
  7.7 0.7 copy-start.4
  8.3 0.7 copy-start.5
  9.0 0.7 copy-start.6
  32.2 3.6 %copy-start.1 = (f32[64,40,800]{2,1,0:T(8,128)S(1)}, f32[64,40,800]{2,1,0:T(8,128)}, u32[]{:S(2)}) copy-start(f32[64,40,800]{2,1,0:T(8,128)} %v_ref.1) | copy-start | bytes 24576004
  45.3 3.2 %copy-start = (f32[16,40,3200]{2,1,0:T(8,128)}, f32[16,40,3200]{2,1,0:T(8,128)S(1)}, u32[]{:S(2)}) copy-start(f32[16,40,3200]{2,1,0:T(8,128)S(1)} %shard_map.56) | copy-start | bytes 24576004
  49.3 123.2 %all-to-all-start.1 = ((f32[16,40,3200]{2,1,0:T(8,128)}), f32[16,40,3200]{2,1,0:T(8,128)}, u32[]{:S(2)}, u32[]{:S(2)}) async-start(f32[16,40,3200]{2,1,0:T(8,128)} %copy-done), calls=%async_computation.1 | async-start | bytes 16384000 | tf_op jit(solution)/shard_map/all_to_all | solution.py:218
  172.5 3.1 %copy-start.2 = (f32[128,56,256]{2,1,0:T(8,128)S(1)}, f32[128,56,256]{2,1,0:T(8,128)}, u32[]{:S(2)}) copy-start(f32[128,56,256]{2,1,0:T(8,128)} %all-gather.3.cloned.1.call-done) | copy-start | bytes 22020100
  194.5 4.5 %collective-permute-start = (f32[16,80,128]{2,1,0:T(8,128)S(1)}, f32[16,80,128]{2,1,0:T(8,128)S(1)}, u32[]{:S(2)}, u32[]{:S(2)}) collective-permute-start(f32[16,80,128]{2,1,0:T(8,128)S(1)} %dynamic-slice_bitcast_fusion), channel_id=1, source_target_pairs={{0,1},{1,0},{2,3},{3,2},{4,5},{5,4},{6,7},{7,6},{8,9},{9,8},{10,11... | collective-permute-start | bytes 1966088 | tf_op jit(solution)/shard_map/ppermute | solution.py:240
Sparse Core Ops, SparseCore 0:
  32.4 84.4 all-gather.2

commit v4 on v3

v4 whole, which is shorter than its diff:
```python
import functools

import jax
import jax.numpy as jnp
from jax import lax
from jax.experimental import pallas as pl
from jax.experimental.pallas import tpu as pltpu
from jax.sharding import Mesh, PartitionSpec as P

RD = 2
PLANE = ("y", "x")
TILE = ("y", "z", "x")
LANES = 128
PITCH = 64
PADDED = 56
VMEM = 56 * 1024 * 1024
FIRST = 56


def pack_kernel(part, tiles, shape, map_ref, cd_ref, res_ref, t_ref, out_ref):
    size_y, size_z, size_x = shape
    square = (LANES, LANES)
    row = lax.broadcasted_iota(jnp.int32, square, 0)
    at_x, at_z, at_y = row % size_x, row // size_x % size_z, row // (size_x * size_z)
    slot = ((at_z * size_y + at_y) * size_x + at_x).astype(jnp.float32)
    ids = jnp.transpose(jnp.broadcast_to(map_ref[...].astype(jnp.float32), square))
    match = ids[:, :tiles] == cd_ref[...].astype(jnp.float32)
    owner = jnp.sum(jnp.where(match, slot[:, :tiles], 0.0), axis=0, keepdims=True)
    ids = jnp.concatenate([owner, res_ref[...].astype(jnp.float32)], axis=1)
    tail = jnp.zeros((PADDED - part, t_ref.shape[1]), jnp.float32)
    for c in range(out_ref.shape[0]):
        out_ref[c, :part, :] = t_ref[c * part : (c + 1) * part, :]
        out_ref[c, part:, :] = tail
        out_ref[c, part : part + 1, : 2 * tiles] = ids


def pack(tile_map, cd_ids, res_ids, turned, cell, shape):
    depth, wide = turned.shape
    part = depth // cell
    tiles = cd_ids.shape[0]
    return pl.pallas_call(
        functools.partial(pack_kernel, part, tiles, shape),
        out_shape=jax.ShapeDtypeStruct((cell, PADDED, wide), jnp.float32),
        compiler_params=pltpu.CompilerParams(vmem_limit_bytes=VMEM),
        cost_estimate=pl.CostEstimate(flops=0, bytes_accessed=depth * wide * 8, transcendentals=0),
    )(tile_map[None], cd_ids[None], res_ids[None], turned)


def cut_kernel(part, spans, v_ref, *out_refs):
    depth = v_ref.shape[2]
    lane = lax.broadcasted_iota(jnp.int32, (8, LANES), 1)
    full = depth // LANES

    def source(h, q):
        if q < full:
            return v_ref[h, :, q * LANES : (q + 1) * LANES]
        rest = v_ref[h, :, full * LANES : depth]
        return jnp.concatenate([rest, jnp.zeros((8, LANES - rest.shape[1]), rest.dtype)], axis=1)

    for (begin, count), out_ref in zip(spans, out_refs, strict=True):
        for c in range(out_ref.shape[0]):
            rolled = {}
            for j in range(out_ref.shape[2] // LANES):
                made = None
                at = j * LANES
                while at < min((j + 1) * LANES, count * part):
                    h, v = divmod(at, part)
                    q, o = divmod(c * part + v, LANES)
                    run = min(part - v, LANES - o, (j + 1) * LANES - at)
                    key = (h, q)
                    if key not in rolled:
                        shift = (part * (h - c)) % LANES
                        value = source(begin + h, q)
                        rolled[key] = pltpu.roll(value, shift, 1) if shift else value
                    made = rolled[key] if made is None else jnp.where(lane >= at - j * LANES, rolled[key], made)
                    at += run
                out_ref[c, :, j * LANES : (j + 1) * LANES] = made


def cut(integrals, cells, spans):
    tiles, rows, depth = integrals.shape
    part = depth // cells
    widths = [pl.cdiv(count * part, LANES) * LANES for _, count in spans]
    return pl.pallas_call(
        functools.partial(cut_kernel, part, spans),
        grid=(rows // 8,),
        in_specs=[pl.BlockSpec((tiles, 8, depth), lambda i: (0, i, 0))],
        out_specs=[pl.BlockSpec((cells, 8, width), lambda i: (0, i, 0)) for width in widths],
        out_shape=[jax.ShapeDtypeStruct((cells, rows, width), jnp.float32) for width in widths],
        compiler_params=pltpu.CompilerParams(vmem_limit_bytes=VMEM),
        cost_estimate=pl.CostEstimate(flops=0, bytes_accessed=tiles * rows * depth * 8, transcendentals=0),
    )(integrals)


def split_kernel(part, t_ref, high_ref, low_ref):
    row = lax.broadcasted_iota(jnp.int32, (PADDED, t_ref.shape[2]), 0)
    for s in range(t_ref.shape[0]):
        value = jnp.where(row < part, t_ref[s], 0.0)
        value = jnp.concatenate([value, jnp.zeros((PITCH - PADDED, value.shape[1]), value.dtype)], axis=0)
        high = value.astype(jnp.bfloat16)
        high_ref[s] = high
        low_ref[s] = (value - high.astype(jnp.float32)).astype(jnp.bfloat16)


def split(held, part):
    peers, rows, wide = held.shape
    block = 16
    shape = jax.ShapeDtypeStruct((peers, PITCH, wide), jnp.bfloat16)
    return pl.pallas_call(
        functools.partial(split_kernel, part),
        grid=(peers // block,),
        in_specs=[pl.BlockSpec((block, rows, wide), lambda i: (i, 0, 0))],
        out_specs=[pl.BlockSpec((block, PITCH, wide), lambda i: (i, 0, 0))] * 2,
        out_shape=(shape, shape),
        compiler_params=pltpu.CompilerParams(vmem_limit_bytes=VMEM),
        cost_estimate=pl.CostEstimate(flops=0, bytes_accessed=peers * wide * 480, transcendentals=0),
    )(held)


def ladder_kernel(part, span, step, meta_ref, v_ref, high_ref, low_ref, *refs):
    d = pl.program_id(0)
    before_ref, out_ref = refs if len(refs) == 2 else (None, refs[0])
    rows = v_ref.shape[1]
    wide = high_ref.shape[2]
    begin, count = span
    tiles = meta_ref.shape[1] // 2
    lane = lax.broadcasted_iota(jnp.int32, (rows, LANES), 1)
    lane_row = lax.broadcasted_iota(jnp.int32, (1, LANES), 1)

    def piece(h):
        q, o = divmod(part * h, LANES)
        base = PITCH * (h % 2)
        shift = (base - o) % LANES
        first = v_ref[0, :, q * LANES : (q + 1) * LANES]
        first = pltpu.roll(first, shift, 1) if shift else first
        if o + part <= LANES:
            return first
        second = v_ref[0, :, (q + 1) * LANES : (q + 2) * LANES]
        second = pltpu.roll(second, shift, 1) if shift else second
        return jnp.where(lane < base + LANES - o, first, second)

    def is_zeroth(h):
        return (1 - meta_ref[d, tiles + begin + h]).astype(jnp.float32)

    total = jnp.zeros((4 * rows, wide), jnp.float32)
    minor = jnp.zeros((2 * rows, wide), jnp.float32)
    for g in range(0, count, step):
        both = []
        for h in range(g, g + step, 2):
            value = jnp.where(lane < PITCH, piece(h), piece(h + 1))
            zeroth = value * jnp.where(lane_row < PITCH, is_zeroth(h), is_zeroth(h + 1))
            value = jnp.concatenate([zeroth, value - zeroth], axis=0)
            rest = value - value.astype(jnp.bfloat16).astype(jnp.float32)
            both.append(jnp.concatenate([value, rest], axis=0).astype(jnp.bfloat16))
        both = jnp.concatenate(both, axis=1)
        at = [meta_ref[d, begin + h] for h in range(g, g + step)]
        t_high = jnp.concatenate([high_ref[s] for s in at], axis=0)
        t_low = jnp.concatenate([low_ref[s] for s in at], axis=0)
        total += jnp.dot(both, t_high, preferred_element_type=jnp.float32)
        minor += jnp.dot(both[: 2 * rows], t_low, preferred_element_type=jnp.float32)
    total = total[: 2 * rows] + total[2 * rows :] + minor
    for k in range(out_ref.shape[0]):
        value = total[:, k * LANES : (k + 1) * LANES]
        out_ref[k, 0] = value if before_ref is None else before_ref[k, 0] + value


def ladder(meta, got, high, low, part, span, step, before=None):
    cell, rows, width = got.shape
    peers, _, wide = high.shape
    cores = wide // LANES
    whole = pl.BlockSpec((peers, PITCH, wide), lambda d, meta: (0, 0, 0), pipeline_mode=pl.Buffered(1))
    sums = pl.BlockSpec((cores, 1, RD * rows, LANES), lambda d, meta: (0, d, 0, 0))
    return pl.pallas_call(
        functools.partial(ladder_kernel, part, span, step),
        grid_spec=pltpu.PrefetchScalarGridSpec(
            num_scalar_prefetch=1,
            grid=(cell,),
            in_specs=[pl.BlockSpec((1, rows, width), lambda d, meta: (d, 0, 0)), whole, whole]
            + ([] if before is None else [sums]),
            out_specs=sums,
        ),
        out_shape=jax.ShapeDtypeStruct((cores, cell, RD * rows, LANES), jnp.float32),
        compiler_params=pltpu.CompilerParams(vmem_limit_bytes=VMEM),
        cost_estimate=pl.CostEstimate(
            flops=12 * RD * rows * cell * span[1] * PITCH * wide, bytes_accessed=4 * got.size + 4 * high.size, transcendentals=0
        ),
    )(meta, got, high, low, *(() if before is None else (before,)))


def exchange(value, axes):
    return lax.all_to_all(value, axes, split_axis=0, concat_axis=0, tiled=True)


def body(amplitudes, integrals, tile_map, cd_ids, res_ids):
    cell = lax.axis_size(PLANE)
    tiles, rows, depth = integrals.shape
    wide = amplitudes.shape[1]
    part = depth // cell
    peers = tile_map.shape[0]
    shape = tuple(lax.axis_size(a) for a in TILE)
    spans = ((0, FIRST), (FIRST, tiles - FIRST))
    own = exchange(pack(tile_map, cd_ids, res_ids, amplitudes[0].T, cell, shape), PLANE)
    sent, late = cut(integrals, cell, spans)
    meta = own[:, part, : 2 * tiles].astype(jnp.int32)
    own, sent, late = lax.optimization_barrier((own, sent, late))
    shared = lax.all_gather(own, "z")
    sent, meta, core = lax.optimization_barrier((sent, meta, lax.axis_index("slab")))
    got = exchange(sent, PLANE)
    got, late, shared, meta, core = lax.optimization_barrier((got, late, shared, meta, core))
    later = exchange(late, PLANE)
    high, low = split(shared.reshape(peers, PADDED, wide), part)
    sums = ladder(meta, got, high, low, part, spans[0], 8)
    sums = ladder(meta, later, high, low, part, spans[1], 8, sums)
    mine = lax.dynamic_index_in_dim(sums, core, 0, keepdims=False)
    other = lax.dynamic_index_in_dim(sums, 1 - core, 0, keepdims=False)
    mine += lax.ppermute(other, "slab", [(0, 1), (1, 0)])
    back = exchange(mine, PLANE)
    return jnp.sum(back, axis=0).reshape(RD, rows, LANES)


def solution(mesh):
    grid = Mesh(mesh.devices.reshape(4, 8, 4, 2), TILE + ("slab",))
    placed = (P(TILE, None, "slab"), P(TILE, None, "slab"), P(), P(TILE), P(TILE))
    return jax.shard_map(
        body, mesh=grid, in_specs=placed, out_specs=P(TILE, None, "slab"), check_vma=False
    )
```

time: 225 us -> 204 us (0.907)
  waiting for transfers between devices: 120 us -> 4.9 us
  blocking collectives: 39.7 us -> 106 us
  Pallas kernels: 28.5 us -> 57.1 us
  local copies, waits for them, and re-layouts: 13.9 us -> 3.99 us
  starting transfers between devices: 7.53 us -> 15 us
    all_to_all x1 -> x2, waiting for transfers between devices: 118 us -> 3.16 us  [exchange(): return lax.all_to_all(value, axes, split_axis=0, concat_axis=0, tiled=True)]
    all_to_all x2, blocking collectives: 39.7 us -> 106 us  [exchange(): return lax.all_to_all(value, axes, split_axis=0, concat_axis=0, tiled=True)]
    pallas_call x2 -> x3, Pallas kernels: 27.3 us -> 46.1 us  [the longest x2 34.7 us: ladder(): pl.pallas_call(functools.partial(ladder_kernel, part, span, step), grid_s...]
    unnamed x14 -> x4, local copies, waits for them, and re-layouts: 13 us -> 2.01 us
    pallas_call x1, Pallas kernels: 1.04 us -> 8.75 us  [split(): pl.pallas_call(functools.partial(split_kernel, part), grid=(peers // bloc...]
    all_to_all x1 -> x2, starting transfers between devices: 4.75 us -> 11.3 us  [exchange(): return lax.all_to_all(value, axes, split_axis=0, concat_axis=0, tiled=True)]
  transfers between devices with their start and end apart: 3 -> 4, of which waited for: 2 -> 2; matrix products, arithmetic and copies ran while one was open for 0% -> 1% of each run, Pallas kernels for 4% -> 20%
where the time goes in v4:
time: 204 us; the launch traced here: 203 us
  blocking collectives  106 us (52%)
  Pallas kernels  57.1 us (28%)
  starting transfers between devices  15 us (7%)
  between operations  13.4 us (7%)
  waiting for transfers between devices  4.9 us (2%)
  local copies, waits for them, and re-layouts  3.99 us (2%)
  other arithmetic  2.41 us (1%)
    all_to_all x2, blocking collectives, exchange(): return lax.all_to_all(value, axes, split_axis=0, concat_axis=0, tiled=True)  106 us
    pallas_call x2, Pallas kernels, ladder(): pl.pallas_call(functools.partial(ladder_kernel, part, span, step), grid_s...  34.7 us
    pallas_call x1, Pallas kernels, cut(): pl.pallas_call(functools.partial(cut_kernel, part, spans), grid=(rows //...  11.4 us
    all_to_all x2, starting transfers between devices, exchange(): return lax.all_to_all(value, axes, split_axis=0, concat_axis=0, tiled=True)  11.3 us
    pallas_call x1, Pallas kernels, split(): pl.pallas_call(functools.partial(split_kernel, part), grid=(peers // bloc...  8.75 us
  transfers between devices with their start and end apart: 4, of which 2 were waited for; matrix products, arithmetic and copies ran while one was open for 1% of the time, Pallas kernels for 20%

profile of v4, /device:TPU:1, one launch (start us, length us, event | category | flops | bytes accessed | tf_op | source)
XLA Modules:
  0.0 202.6 jit_solution(14373240197803690210)
XLA Ops:
  6.5 2.3 %shard_map.55 = f32[16,56,256]{2,1,0:T(8,128)} custom-call(s32[1,128]{1,0:T(1,128)} %bitcast.18, s32[1,64]{1,0:T(1,128)} %bitcast.19, s32[1,64]{1,0:T(1,128)} %bitcast.20, f32[800,256]{1,0:T(8,128)} %bitcast.16), custom_call_target="tpu_custom_call" | custom-call | bytes 1638400 | tf_op jit(solution)/shard_map/pallas_call | solution.py:41
  8.8 7.6 %all-to-all-start = ((f32[16,56,256]{2,1,0:T(8,128)}), f32[16,56,256]{2,1,0:T(8,128)S(1)}, u32[]{:S(2)}, u32[]{:S(2)}) async-start(f32[16,56,256]{2,1,0:T(8,128)} %shard_map.55), calls=%async_computation | async-start | bytes 1835008 | tf_op jit(solution)/shard_map/all_to_all | solution.py:191
  16.4 0.0 all-gather.3.cloned.1.call-start
  16.4 11.4 %shard_map.56 = (f32[16,40,2816]{2,1,0:T(8,128)}, f32[16,40,512]{2,1,0:T(8,128)}) custom-call(f32[64,40,800]{2,1,0:T(8,128)} %v_ref.1), custom_call_target="tpu_custom_call" | custom-call | bytes 16384000 | tf_op jit(solution)/shard_map/pallas_call | solution.py:84
  27.8 3.2 %all-to-all-done = f32[16,56,256]{2,1,0:T(8,128)S(1)} async-done(((f32[16,56,256]{2,1,0:T(8,128)}), f32[16,56,256]{2,1,0:T(8,128)S(1)}, u32[]{:S(2)}, u32[]{:S(2)}) %all-to-all-start) | async-done | bytes 917536 | tf_op jit(solution)/shard_map/all_to_all | solution.py:191
  31.0 0.0 copy-start.1
  31.0 1.0 copy-done.1
  31.9 0.0 all-gather.3.cloned.1.call-update
  32.0 0.8 slice.4
  32.8 0.6 convert_bitcast_fusion.meta_ref
  33.4 86.7 %all_to_all.20.v_ref = f32[16,40,2816]{2,1,0:T(8,128)} all-to-all(f32[16,40,2816]{2,1,0:T(8,128)} %get-tuple-element.23), channel_id=1, replica_groups=mesh['y'=4,'z'=8,'x'=4,'slab'=2] {'y','x'}, dimensions={0} | all-to-all | bytes 14417920 | tf_op jit(solution)/shard_map/all_to_all | solution.py:191
  120.1 0.0 all-gather.3.cloned.1.call-done
  120.1 3.7 %all-to-all-start.2 = ((f32[16,40,512]{2,1,0:T(8,128)}), f32[16,40,512]{2,1,0:T(8,128)S(1)}, u32[]{:S(2)}, u32[]{:S(2)}) async-start(f32[16,40,512]{2,1,0:T(8,128)} %get-tuple-element.29), calls=%async_computation.2 | async-start | bytes 2621440 | tf_op jit(solution)/shard_map/all_to_all | solution.py:191
  123.8 8.8 %shard_map.57 = (bf16[128,64,256]{2,1,0:T(8,128)(2,1)}, bf16[128,64,256]{2,1,0:T(8,128)(2,1)}) custom-call(f32[128,56,256]{2,1,0:T(8,128)} %all-gather.3.cloned.1.call-done), custom_call_target="tpu_custom_call" | custom-call | bytes 15728640 | tf_op jit(solution)/shard_map/pallas_call | solution.py:109
  132.6 19.7 %shard_map.58.refs_0_ = f32[2,16,80,128]{3,2,1,0:T(8,128)} custom-call(s32[16,128]{1,0:T(8,128)} %convert_bitcast_fusion.meta_ref, f32[16,40,2816]{2,1,0:T(8,128)} %all_to_all.20.v_ref, bf16[128,64,256]{2,1,0:T(8,128)(2,1)} %get-tuple-element.31.high_ref, bf16[128,64,256]{2,1,0:T(8,128)(2,1)} %get-tuple-element.32.low_ref), custom_call_target="tpu_custom_call" | custom-call | flops 14092861440 | bytes 15597568 | tf_op jit(solution)/shard_map/pallas_call | solution.py:173
  152.3 0.0 all-to-all-done.2.v_ref
  152.3 0.0 copy-start
  152.3 1.1 copy-done
  153.3 15.0 %shard_map.59 = f32[2,16,80,128]{3,2,1,0:T(8,128)} custom-call(s32[16,128]{1,0:T(8,128)} %convert_bitcast_fusion.meta_ref, f32[16,40,512]{2,1,0:T(8,128)} %copy-done, bf16[128,64,256]{2,1,0:T(8,128)(2,1)} %get-tuple-element.31.high_ref, bf16[128,64,256]{2,1,0:T(8,128)(2,1)} %get-tuple-element.32.low_ref, f32[2,16,80,128]{3,2,1,0:T(8,128)} %shard_map.58.refs_0_), custom_call_target="tpu_custom_call" | custom-call | flops 2013265920 | bytes 9699328 | tf_op jit(solution)/shard_map/pallas_call | solution.py:173
  168.3 1.1 dynamic-slice_bitcast_fusion
  169.5 3.7 %collective-permute-start = (f32[16,80,128]{2,1,0:T(8,128)S(1)}, f32[16,80,128]{2,1,0:T(8,128)S(1)}, u32[]{:S(2)}, u32[]{:S(2)}) collective-permute-start(f32[16,80,128]{2,1,0:T(8,128)S(1)} %dynamic-slice_bitcast_fusion), channel_id=1, source_target_pairs={{0,1},{1,0},{2,3},{3,2},{4,5},{5,4},{6,7},{7,6},{8,9},{9,8},{10,11... | collective-permute-start | bytes 1966088 | tf_op jit(solution)/shard_map/ppermute | solution.py:216
  173.2 1.7 collective-permute-done
  174.9 1.2 bitcast_add_fusion
  176.0 19.1 %all_to_all.21 = f32[16,80,128]{2,1,0:T(8,128)S(1)} all-to-all(f32[16,80,128]{2,1,0:T(8,128)S(1)} %bitcast_add_fusion), channel_id=1, replica_groups=mesh['y'=4,'z'=8,'x'=4,'slab'=2] {'y','x'}, dimensions={0} | all-to-all | bytes 1310720 | tf_op jit(solution)/shard_map/all_to_all | solution.py:191
  195.1 0.7 reduce_sum.9
Async XLA Ops:
  8.8 22.2 %all-to-all-start = ((f32[16,56,256]{2,1,0:T(8,128)}), f32[16,56,256]{2,1,0:T(8,128)S(1)}, u32[]{:S(2)}, u32[]{:S(2)}) async-start(f32[16,56,256]{2,1,0:T(8,128)} %shard_map.55), calls=%async_computation | async-start | bytes 1835008 | tf_op jit(solution)/shard_map/all_to_all | solution.py:191
  16.4 103.7 %all-gather.3.cloned.1.call-start = ((), (), s32[]{:S(2)}) async-start(), calls=%async_computation.4 | async-start | bytes 8257536 | tf_op jit(solution)/shard_map/all_gather | solution.py:206
  31.0 1.0 copy-start.1
  120.1 32.2 %all-to-all-start.2 = ((f32[16,40,512]{2,1,0:T(8,128)}), f32[16,40,512]{2,1,0:T(8,128)S(1)}, u32[]{:S(2)}, u32[]{:S(2)}) async-start(f32[16,40,512]{2,1,0:T(8,128)} %get-tuple-element.29), calls=%async_computation.2 | async-start | bytes 2621440 | tf_op jit(solution)/shard_map/all_to_all | solution.py:191
  152.3 1.1 copy-start
  169.5 5.4 %collective-permute-start = (f32[16,80,128]{2,1,0:T(8,128)S(1)}, f32[16,80,128]{2,1,0:T(8,128)S(1)}, u32[]{:S(2)}, u32[]{:S(2)}) collective-permute-start(f32[16,80,128]{2,1,0:T(8,128)S(1)} %dynamic-slice_bitcast_fusion), channel_id=1, source_target_pairs={{0,1},{1,0},{2,3},{3,2},{4,5},{5,4},{6,7},{7,6},{8,9},{9,8},{10,11... | collective-permute-start | bytes 1966088 | tf_op jit(solution)/shard_map/ppermute | solution.py:216
Sparse Core Ops, SparseCore 0:
  32.1 84.6 all-gather.2

commit v5 on v4

--- a/solution.py
+++ b/solution.py
@@ -92,38 +92,9 @@
     )(integrals)
 
 
-def split_kernel(part, t_ref, high_ref, low_ref):
-    row = lax.broadcasted_iota(jnp.int32, (PADDED, t_ref.shape[2]), 0)
-    for s in range(t_ref.shape[0]):
-        value = jnp.where(row < part, t_ref[s], 0.0)
-        value = jnp.concatenate([value, jnp.zeros((PITCH - PADDED, value.shape[1]), value.dtype)], axis=0)
-        high = value.astype(jnp.bfloat16)
-        high_ref[s] = high
-        low_ref[s] = (value - high.astype(jnp.float32)).astype(jnp.bfloat16)
-
-
-def split(held, part):
-    peers, rows, wide = held.shape
-    block = 16
-    shape = jax.ShapeDtypeStruct((peers, PITCH, wide), jnp.bfloat16)
-    return pl.pallas_call(
-        functools.partial(split_kernel, part),
-        grid=(peers // block,),
-        in_specs=[pl.BlockSpec((block, rows, wide), lambda i: (i, 0, 0))],
-        out_specs=[pl.BlockSpec((block, PITCH, wide), lambda i: (i, 0, 0))] * 2,
-        out_shape=(shape, shape),
-        compiler_params=pltpu.CompilerParams(vmem_limit_bytes=VMEM),
-        cost_estimate=pl.CostEstimate(flops=0, bytes_accessed=peers * wide * 480, transcendentals=0),
-    )(held)
-
-
-def ladder_kernel(part, span, step, meta_ref, v_ref, high_ref, low_ref, *refs):
-    d = pl.program_id(0)
-    before_ref, out_ref = refs if len(refs) == 2 else (None, refs[0])
-    rows = v_ref.shape[1]
+def contract(part, span, step, tiles, own, load, rows, high_ref, low_ref):
     wide = high_ref.shape[2]
     begin, count = span
-    tiles = meta_ref.shape[1] // 2
     lane = lax.broadcasted_iota(jnp.int32, (rows, LANES), 1)
     lane_row = lax.broadcasted_iota(jnp.int32, (1, LANES), 1)
 
@@ -131,16 +102,16 @@
         q, o = divmod(part * h, LANES)
         base = PITCH * (h % 2)
         shift = (base - o) % LANES
-        first = v_ref[0, :, q * LANES : (q + 1) * LANES]
+        first = load(q)
         first = pltpu.roll(first, shift, 1) if shift else first
         if o + part <= LANES:
             return first
-        second = v_ref[0, :, (q + 1) * LANES : (q + 2) * LANES]
+        second = load(q + 1)
         second = pltpu.roll(second, shift, 1) if shift else second
         return jnp.where(lane < base + LANES - o, first, second)
 
     def is_zeroth(h):
-        return (1 - meta_ref[d, tiles + begin + h]).astype(jnp.float32)
+        return (1 - own(tiles + begin + h)).astype(jnp.float32)
 
     total = jnp.zeros((4 * rows, wide), jnp.float32)
     minor = jnp.zeros((2 * rows, wide), jnp.float32)
@@ -153,38 +124,137 @@
             rest = value - value.astype(jnp.bfloat16).astype(jnp.float32)
             both.append(jnp.concatenate([value, rest], axis=0).astype(jnp.bfloat16))
         both = jnp.concatenate(both, axis=1)
-        at = [meta_ref[d, begin + h] for h in range(g, g + step)]
+        at = [own(begin + h) for h in range(g, g + step)]
         t_high = jnp.concatenate([high_ref[s] for s in at], axis=0)
         t_low = jnp.concatenate([low_ref[s] for s in at], axis=0)
         total += jnp.dot(both, t_high, preferred_element_type=jnp.float32)
         minor += jnp.dot(both[: 2 * rows], t_low, preferred_element_type=jnp.float32)
-    total = total[: 2 * rows] + total[2 * rows :] + minor
+    return total[: 2 * rows] + total[2 * rows :] + minor
+
+
+def first_kernel(part, span, step, meta_ref, v_ref, t_hbm, out_ref, high_hbm, low_hbm, t_ref, high_ref, low_ref, in_sems, out_sems):
+    d = pl.program_id(0)
+    peers = t_ref.shape[0]
+    chunks = in_sems.shape[0]
+    each = peers // chunks
+    row = lax.broadcasted_iota(jnp.int32, t_ref.shape[1:], 0)
+
+    def fetch(k):
+        at = pl.ds(k * each, each)
+        return pltpu.make_async_copy(t_hbm.at[at], t_ref.at[at], in_sems.at[k])
+
+    keep_high = pltpu.make_async_copy(high_ref, high_hbm, out_sems.at[0])
+    keep_low = pltpu.make_async_copy(low_ref, low_hbm, out_sems.at[1])
+
+    @pl.when(d == 0)
+    def _():
+        for k in range(chunks):
+            fetch(k).start()
+        for k in range(chunks):
+            fetch(k).wait()
+
+            def split(i, _, k=k):
+                s = k * each + i
+                value = jnp.where(row < part, t_ref[s], 0.0)
+                value = jnp.concatenate([value, jnp.zeros((PITCH - PADDED, value.shape[1]), value.dtype)], axis=0)
+                high = value.astype(jnp.bfloat16)
+                high_ref[s] = high
+                low_ref[s] = (value - high.astype(jnp.float32)).astype(jnp.bfloat16)
+                return 0
+
+            lax.fori_loop(0, each, split, 0, unroll=4)
+        keep_high.start()
+        keep_low.start()
+
+    total = contract(
+        part, span, step, meta_ref.shape[1] // 2, lambda i: meta_ref[d, i],
+        lambda q: v_ref[0, :, q * LANES : (q + 1) * LANES], v_ref.shape[1], high_ref, low_ref,
+    )
     for k in range(out_ref.shape[0]):
-        value = total[:, k * LANES : (k + 1) * LANES]
-        out_ref[k, 0] = value if before_ref is None else before_ref[k, 0] + value
-
-
-def ladder(meta, got, high, low, part, span, step, before=None):
+        out_ref[k, 0] = total[:, k * LANES : (k + 1) * LANES]
+
+    @pl.when(d == pl.num_programs(0) - 1)
+    def _():
+        keep_high.wait()
+        keep_low.wait()
+
+
+def first_ladder(meta, got, held, part, span, step):
+    cell, rows, width = got.shape
+    peers, padded, wide = held.shape
+    cores = wide // LANES
+    chunks = 8
+    anywhere = pl.BlockSpec(memory_space=pl.ANY)
+    half = jax.ShapeDtypeStruct((peers, PITCH, wide), jnp.bfloat16)
+    return pl.pallas_call(
+        functools.partial(first_kernel, part, span, step),
+        grid_spec=pltpu.PrefetchScalarGridSpec(
+            num_scalar_prefetch=1,
+            grid=(cell,),
+            in_specs=[pl.BlockSpec((1, rows, width), lambda d, meta: (d, 0, 0)), anywhere],
+            out_specs=[pl.BlockSpec((cores, 1, RD * rows, LANES), lambda d, meta: (0, d, 0, 0)), anywhere, anywhere],
+            scratch_shapes=[
+                pltpu.VMEM((peers, padded, wide), jnp.float32),
+                pltpu.VMEM((peers, PITCH, wide), jnp.bfloat16),
+                pltpu.VMEM((peers, PITCH, wide), jnp.bfloat16),
+                pltpu.SemaphoreType.DMA((chunks,)),
+                pltpu.SemaphoreType.DMA((2,)),
+            ],
+        ),
+        out_shape=(jax.ShapeDtypeStruct((cores, cell, RD * rows, LANES), jnp.float32), half, half),
+        compiler_params=pltpu.CompilerParams(vmem_limit_bytes=VMEM),
+        cost_estimate=pl.CostEstimate(
+            flops=12 * RD * rows * cell * span[1] * PITCH * wide, bytes_accessed=4 * got.size + 8 * held.size, transcendentals=0
+        ),
+    )(meta, got, held)
+
+
+def last_kernel(part, span, step, meta_ref, core_ref, v_ref, high_ref, low_ref, before_ref, mine_ref, other_ref):
+    per = v_ref.shape[0]
+    first = pl.program_id(0) * per
+    is_first = core_ref[0] == 0
+
+    def block(i, _):
+        total = contract(
+            part, span, step, meta_ref.shape[1] // 2, lambda k: meta_ref[first + i, k],
+            lambda q: v_ref[i, :, q * LANES : (q + 1) * LANES], v_ref.shape[1], high_ref, low_ref,
+        )
+        lower = before_ref[0, i] + total[:, :LANES]
+        upper = before_ref[1, i] + total[:, LANES:]
+        mine_ref[i] = jnp.where(is_first, lower, upper)
+        other_ref[i] = jnp.where(is_first, upper, lower)
+        return 0
+
+    lax.fori_loop(0, per, block, 0)
+
+
+def last_ladder(meta, core, got, high, low, before, part, span, step):
     cell, rows, width = got.shape
     peers, _, wide = high.shape
     cores = wide // LANES
-    whole = pl.BlockSpec((peers, PITCH, wide), lambda d, meta: (0, 0, 0), pipeline_mode=pl.Buffered(1))
-    sums = pl.BlockSpec((cores, 1, RD * rows, LANES), lambda d, meta: (0, d, 0, 0))
-    return pl.pallas_call(
-        functools.partial(ladder_kernel, part, span, step),
+    per = cell // 2
+    whole = pl.BlockSpec((peers, PITCH, wide), lambda d, *_: (0, 0, 0), pipeline_mode=pl.Buffered(1))
+    sums = pl.BlockSpec((per, RD * rows, LANES), lambda d, *_: (d, 0, 0))
+    shape = jax.ShapeDtypeStruct((cell, RD * rows, LANES), jnp.float32)
+    return pl.pallas_call(
+        functools.partial(last_kernel, part, span, step),
         grid_spec=pltpu.PrefetchScalarGridSpec(
-            num_scalar_prefetch=1,
-            grid=(cell,),
-            in_specs=[pl.BlockSpec((1, rows, width), lambda d, meta: (d, 0, 0)), whole, whole]
-            + ([] if before is None else [sums]),
-            out_specs=sums,
-        ),
-        out_shape=jax.ShapeDtypeStruct((cores, cell, RD * rows, LANES), jnp.float32),
+            num_scalar_prefetch=2,
+            grid=(cell // per,),
+            in_specs=[
+                pl.BlockSpec((per, rows, width), lambda d, *_: (d, 0, 0)),
+                whole,
+                whole,
+                pl.BlockSpec((cores, per, RD * rows, LANES), lambda d, *_: (0, d, 0, 0)),
+            ],
+            out_specs=[sums, sums],
+        ),
+        out_shape=(shape, shape),
         compiler_params=pltpu.CompilerParams(vmem_limit_bytes=VMEM),
         cost_estimate=pl.CostEstimate(
             flops=12 * RD * rows * cell * span[1] * PITCH * wide, bytes_accessed=4 * got.size + 4 * high.size, transcendentals=0
         ),
-    )(meta, got, high, low, *(() if before is None else (before,)))
+    )(meta, core, got, high, low, before)
 
 
 def exchange(value, axes):
@@ -201,18 +271,16 @@
     spans = ((0, FIRST), (FIRST, tiles - FIRST))
     own = exchange(pack(tile_map, cd_ids, res_ids, amplitudes[0].T, cell, shape), PLANE)
     sent, late = cut(integrals, cell, spans)
-    meta = own[:, part, : 2 * tiles].astype(jnp.int32)
+    ids = own[:, part, : 2 * tiles]
     own, sent, late = lax.optimization_barrier((own, sent, late))
     shared = lax.all_gather(own, "z")
-    sent, meta, core = lax.optimization_barrier((sent, meta, lax.axis_index("slab")))
+    sent, ids, core = lax.optimization_barrier((sent, ids, lax.axis_index("slab")))
     got = exchange(sent, PLANE)
-    got, late, shared, meta, core = lax.optimization_barrier((got, late, shared, meta, core))
+    got, late, shared, ids, core = lax.optimization_barrier((got, late, shared, ids, core))
     later = exchange(late, PLANE)
-    high, low = split(shared.reshape(peers, PADDED, wide), part)
-    sums = ladder(meta, got, high, low, part, spans[0], 8)
-    sums = ladder(meta, later, high, low, part, spans[1], 8, sums)
-    mine = lax.dynamic_index_in_dim(sums, core, 0, keepdims=False)
-    other = lax.dynamic_index_in_dim(sums, 1 - core, 0, keepdims=False)
+    meta = ids.astype(jnp.int32)
+    sums, high, low = first_ladder(meta, got, shared.reshape(peers, PADDED, wide), part, spans[0], 8)
+    mine, other = last_ladder(meta, core[None], later, high, low, sums, part, spans[1], 8)
     mine += lax.ppermute(other, "slab", [(0, 1), (1, 0)])
     back = exchange(mine, PLANE)
     return jnp.sum(back, axis=0).reshape(RD, rows, LANES)

time: 204 us -> 192 us (0.941)
  Pallas kernels: 57.1 us -> 46.3 us
    pallas_call x3 -> x2, Pallas kernels: 43.4 us -> 32.6 us  [the longest x1 22.2 us: first_ladder(): pl.pallas_call(functools.partial(first_kernel, part, span, step), grid_sp...]
  transfers between devices with their start and end apart: 4 -> 4, of which waited for: 2 -> 2; matrix products, arithmetic and copies ran while one was open for 1% -> 0% of each run, Pallas kernels for 20% -> 18%
where the time goes in v5:
time: 192 us; the launch traced here: 191 us
  blocking collectives  106 us (55%)
  Pallas kernels  46.3 us (24%)
  starting transfers between devices  14.9 us (8%)
  between operations  13.4 us (7%)
  waiting for transfers between devices  5.09 us (3%)
  local copies, waits for them, and re-layouts  2.96 us (2%)
  other arithmetic  2.41 us (1%)
    all_to_all x2, blocking collectives, exchange(): return lax.all_to_all(value, axes, split_axis=0, concat_axis=0, tiled=True)  106 us
    pallas_call x1, Pallas kernels, first_ladder(): pl.pallas_call(functools.partial(first_kernel, part, span, step), grid_sp...  22.2 us
    pallas_call x1, Pallas kernels, cut(): pl.pallas_call(functools.partial(cut_kernel, part, spans), grid=(rows //...  11.4 us
    all_to_all x2, starting transfers between devices, exchange(): return lax.all_to_all(value, axes, split_axis=0, concat_axis=0, tiled=True)  11.4 us
    pallas_call x1, Pallas kernels, last_ladder(): pl.pallas_call(functools.partial(last_kernel, part, span, step), grid_spe...  10.4 us
  transfers between devices with their start and end apart: 4, of which 2 were waited for; matrix products, arithmetic and copies ran while one was open for 0% of the time, Pallas kernels for 18%

profile of v5, /device:TPU:1, one launch (start us, length us, event | category | flops | bytes accessed | tf_op | source)
XLA Modules:
  0.0 191.0 jit_solution(848100813408672814)
XLA Ops:
  6.5 2.3 %shard_map.55 = f32[16,56,256]{2,1,0:T(8,128)} custom-call(s32[1,128]{1,0:T(1,128)} %bitcast.15, s32[1,64]{1,0:T(1,128)} %bitcast.16, s32[1,64]{1,0:T(1,128)} %bitcast.17, f32[800,256]{1,0:T(8,128)} %bitcast.13), custom_call_target="tpu_custom_call" | custom-call | bytes 1638400 | tf_op jit(solution)/shard_map/pallas_call | solution.py:41
  8.9 7.6 %all-to-all-start = ((f32[16,56,256]{2,1,0:T(8,128)}), f32[16,56,256]{2,1,0:T(8,128)S(1)}, u32[]{:S(2)}, u32[]{:S(2)}) async-start(f32[16,56,256]{2,1,0:T(8,128)} %shard_map.55), calls=%async_computation | async-start | bytes 1835008 | tf_op jit(solution)/shard_map/all_to_all | solution.py:261
  16.5 0.0 all-gather.3.cloned.1.call-start
  16.5 11.4 %shard_map.56 = (f32[16,40,2816]{2,1,0:T(8,128)}, f32[16,40,512]{2,1,0:T(8,128)}) custom-call(f32[64,40,800]{2,1,0:T(8,128)} %v_ref.1), custom_call_target="tpu_custom_call" | custom-call | bytes 16384000 | tf_op jit(solution)/shard_map/pallas_call | solution.py:84
  27.9 3.1 %all-to-all-done = f32[16,56,256]{2,1,0:T(8,128)S(1)} async-done(((f32[16,56,256]{2,1,0:T(8,128)}), f32[16,56,256]{2,1,0:T(8,128)S(1)}, u32[]{:S(2)}, u32[]{:S(2)}) %all-to-all-start) | async-done | bytes 917536 | tf_op jit(solution)/shard_map/all_to_all | solution.py:261
  31.0 0.0 copy-start.1
  31.0 1.0 copy-done.1
  32.1 0.0 all-gather.3.cloned.1.call-update
  32.1 0.8 slice.4
  32.9 86.7 %all_to_all.20.v_ref = f32[16,40,2816]{2,1,0:T(8,128)} all-to-all(f32[16,40,2816]{2,1,0:T(8,128)} %get-tuple-element.26), channel_id=1, replica_groups=mesh['y'=4,'z'=8,'x'=4,'slab'=2] {'y','x'}, dimensions={0} | all-to-all | bytes 14417920 | tf_op jit(solution)/shard_map/all_to_all | solution.py:261
  119.7 0.0 all-gather.3.cloned.1.call-done
  119.7 0.6 convert_element_type.3.meta_ref
  120.3 3.8 %all-to-all-start.2 = ((f32[16,40,512]{2,1,0:T(8,128)}), f32[16,40,512]{2,1,0:T(8,128)S(1)}, u32[]{:S(2)}, u32[]{:S(2)}) async-start(f32[16,40,512]{2,1,0:T(8,128)} %get-tuple-element.33), calls=%async_computation.2 | async-start | bytes 2621440 | tf_op jit(solution)/shard_map/all_to_all | solution.py:261
  124.1 22.2 %shard_map.57 = (f32[2,16,80,128]{3,2,1,0:T(8,128)}, bf16[128,64,256]{2,1,0:T(8,128)(2,1)}, bf16[128,64,256]{2,1,0:T(8,128)(2,1)}) custom-call(s32[16,128]{1,0:T(8,128)} %convert_element_type.3.meta_ref, f32[16,40,2816]{2,1,0:T(8,128)} %all_to_all.20.v_ref, f32[128,56,256]{2,1,0:T(8,128)} %all-gather.3.cloned.1.call-done), custom_call_target="tpu_custom_call" | custom-call | flops 14092861440 | bytes 21889024 | tf_op jit(solution)/shard_map/pallas_call | solution.py:189
  146.2 0.0 all-to-all-done.2.v_ref
  146.2 0.0 copy-start
  146.3 1.1 copy-done
  147.3 10.4 %shard_map.58 = (f32[16,80,128]{2,1,0:T(8,128)}, f32[16,80,128]{2,1,0:T(8,128)}) custom-call(s32[16,128]{1,0:T(8,128)} %convert_element_type.3.meta_ref, s32[1]{0:T(128)} %bitcast.7.core_ref, f32[16,40,512]{2,1,0:T(8,128)} %copy-done, bf16[128,64,256]{2,1,0:T(8,128)(2,1)} %get-tuple-element.36.high_ref, bf16[128,64,256]{2,1,0:T(8,128)(2,1)} %get-tuple-element.37.low_ref, ...), custom_call_target="tpu_custom_call" | custom-call | flops 2013265920 | bytes 9699328 | tf_op jit(solution)/shard_map/pallas_call | solution.py:239
  157.8 3.5 %collective-permute-start = (f32[16,80,128]{2,1,0:T(8,128)}, f32[16,80,128]{2,1,0:T(8,128)S(1)}, u32[]{:S(2)}, u32[]{:S(2)}) collective-permute-start(f32[16,80,128]{2,1,0:T(8,128)} %get-tuple-element.40), channel_id=1, source_target_pairs={{0,1},{1,0},{2,3},{3,2},{4,5},{5,4},{6,7},{7,6},{8,9},{9,8},{10,11... | collective-permute-start | bytes 1966088 | tf_op jit(solution)/shard_map/ppermute | solution.py:284
  161.3 1.9 %collective-permute-done = f32[16,80,128]{2,1,0:T(8,128)S(1)} collective-permute-done((f32[16,80,128]{2,1,0:T(8,128)}, f32[16,80,128]{2,1,0:T(8,128)S(1)}, u32[]{:S(2)}, u32[]{:S(2)}) %collective-permute-start) | collective-permute-done | bytes 655392 | tf_op jit(solution)/shard_map/ppermute | solution.py:284
  163.2 1.2 add.3
  164.4 19.1 %all_to_all.21 = f32[16,80,128]{2,1,0:T(8,128)S(1)} all-to-all(f32[16,80,128]{2,1,0:T(8,128)S(1)} %add.3), channel_id=1, replica_groups=mesh['y'=4,'z'=8,'x'=4,'slab'=2] {'y','x'}, dimensions={0} | all-to-all | bytes 1310720 | tf_op jit(solution)/shard_map/all_to_all | solution.py:261
  183.5 0.7 reduce_sum.9
Async XLA Ops:
  8.9 22.2 %all-to-all-start = ((f32[16,56,256]{2,1,0:T(8,128)}), f32[16,56,256]{2,1,0:T(8,128)S(1)}, u32[]{:S(2)}, u32[]{:S(2)}) async-start(f32[16,56,256]{2,1,0:T(8,128)} %shard_map.55), calls=%async_computation | async-start | bytes 1835008 | tf_op jit(solution)/shard_map/all_to_all | solution.py:261
  16.5 103.2 %all-gather.3.cloned.1.call-start = ((), (), s32[]{:S(2)}) async-start(), calls=%async_computation.4 | async-start | bytes 8257536 | tf_op jit(solution)/shard_map/all_gather | solution.py:276
  31.0 1.0 copy-start.1
  120.3 26.0 %all-to-all-start.2 = ((f32[16,40,512]{2,1,0:T(8,128)}), f32[16,40,512]{2,1,0:T(8,128)S(1)}, u32[]{:S(2)}, u32[]{:S(2)}) async-start(f32[16,40,512]{2,1,0:T(8,128)} %get-tuple-element.33), calls=%async_computation.2 | async-start | bytes 2621440 | tf_op jit(solution)/shard_map/all_to_all | solution.py:261
  146.2 1.1 copy-start
  157.8 5.5 %collective-permute-start = (f32[16,80,128]{2,1,0:T(8,128)}, f32[16,80,128]{2,1,0:T(8,128)S(1)}, u32[]{:S(2)}, u32[]{:S(2)}) collective-permute-start(f32[16,80,128]{2,1,0:T(8,128)} %get-tuple-element.40), channel_id=1, source_target_pairs={{0,1},{1,0},{2,3},{3,2},{4,5},{5,4},{6,7},{7,6},{8,9},{9,8},{10,11... | collective-permute-start | bytes 1966088 | tf_op jit(solution)/shard_map/ppermute | solution.py:284
Sparse Core Ops, SparseCore 0:
  32.2 84.6 all-gather.2

commit v6 on v1

v6 whole, which is shorter than its diff:
```python
import functools

import jax
import jax.numpy as jnp
from jax import lax
from jax.experimental import pallas as pl
from jax.experimental.pallas import tpu as pltpu
from jax.sharding import Mesh, PartitionSpec as P

RD = 2
PLANE = ("y", "x")
TILE = ("y", "z", "x")
LANES = 128
PITCH = 64
PADDED = 56
VMEM = 56 * 1024 * 1024


def pack_kernel(part, tiles, shape, map_ref, cd_ref, res_ref, t_ref, out_ref):
    size_y, size_z, size_x = shape
    square = (LANES, LANES)
    row = lax.broadcasted_iota(jnp.int32, square, 0)
    at_x, at_z, at_y = row % size_x, row // size_x % size_z, row // (size_x * size_z)
    slot = ((at_z * size_y + at_y) * size_x + at_x).astype(jnp.float32)
    ids = jnp.transpose(jnp.broadcast_to(map_ref[...].astype(jnp.float32), square))
    match = ids[:, :tiles] == cd_ref[...].astype(jnp.float32)
    owner = jnp.sum(jnp.where(match, slot[:, :tiles], 0.0), axis=0, keepdims=True)
    ids = jnp.concatenate([owner, res_ref[...].astype(jnp.float32)], axis=1)
    tail = jnp.zeros((PADDED - part, t_ref.shape[1]), jnp.float32)
    for c in range(out_ref.shape[0]):
        out_ref[c, :part, :] = t_ref[c * part : (c + 1) * part, :]
        out_ref[c, part:, :] = tail
        out_ref[c, part : part + 1, : 2 * tiles] = ids


def pack(tile_map, cd_ids, res_ids, turned, cell, shape):
    depth, wide = turned.shape
    part = depth // cell
    tiles = cd_ids.shape[0]
    return pl.pallas_call(
        functools.partial(pack_kernel, part, tiles, shape),
        out_shape=jax.ShapeDtypeStruct((cell, PADDED, wide), jnp.float32),
        compiler_params=pltpu.CompilerParams(vmem_limit_bytes=VMEM),
        cost_estimate=pl.CostEstimate(flops=0, bytes_accessed=depth * wide * 8, transcendentals=0),
    )(tile_map[None], cd_ids[None], res_ids[None], turned)


def cut_kernel(part, v_ref, out_ref):
    depth = v_ref.shape[2]
    lane = lax.broadcasted_iota(jnp.int32, (8, LANES), 1)
    full = depth // LANES

    def source(h, q):
        if q < full:
            return v_ref[h, :, q * LANES : (q + 1) * LANES]
        rest = v_ref[h, :, full * LANES : depth]
        return jnp.concatenate([rest, jnp.zeros((8, LANES - rest.shape[1]), rest.dtype)], axis=1)

    for c in range(out_ref.shape[0]):
        rolled = {}
        for j in range(out_ref.shape[2] // LANES):
            made = None
            at = j * LANES
            while at < (j + 1) * LANES:
                h, v = divmod(at, part)
                q, o = divmod(c * part + v, LANES)
                run = min(part - v, LANES - o, (j + 1) * LANES - at)
                key = (h, q)
                if key not in rolled:
                    shift = (part * (h - c)) % LANES
                    rolled[key] = pltpu.roll(source(h, q), shift, 1) if shift else source(h, q)
                made = rolled[key] if made is None else jnp.where(lane >= at - j * LANES, rolled[key], made)
                at += run
            out_ref[c, :, j * LANES : (j + 1) * LANES] = made


def cut(integrals, cells):
    tiles, rows, depth = integrals.shape
    part = depth // cells
    return pl.pallas_call(
        functools.partial(cut_kernel, part),
        grid=(rows // 8,),
        in_specs=[pl.BlockSpec((tiles, 8, depth), lambda i: (0, i, 0))],
        out_specs=pl.BlockSpec((cells, 8, tiles * part), lambda i: (0, i, 0)),
        out_shape=jax.ShapeDtypeStruct((cells, rows, tiles * part), jnp.float32),
        compiler_params=pltpu.CompilerParams(vmem_limit_bytes=VMEM),
        cost_estimate=pl.CostEstimate(flops=0, bytes_accessed=tiles * rows * depth * 8, transcendentals=0),
    )(integrals)


def ladder_kernel(
    part, step, ids_ref, core_ref, v_hbm, t_hbm, mine_hbm, other_hbm,
    v_ref, t_ref, high_ref, low_ref, mine_ref, other_ref, t_sems, v_sems, mine_sems, other_sems,
):
    peers, _, wide = t_ref.shape
    cell, rows, _ = v_ref.shape
    tiles = v_ref.shape[2] // part
    chunks = t_sems.shape[0]
    ahead = 4
    each = peers // chunks
    lane = lax.broadcasted_iota(jnp.int32, (rows, LANES), 1)
    lane_row = lax.broadcasted_iota(jnp.int32, (1, LANES), 1)
    whole = part // 8 * 8
    row = lax.broadcasted_iota(jnp.int32, (PADDED - whole, wide), 0)

    def fetch_t(k):
        at = pl.ds(k * each, each)
        return pltpu.make_async_copy(t_hbm.at[at], t_ref.at[at], t_sems.at[k])

    def fetch_v(d):
        return pltpu.make_async_copy(v_hbm.at[d], v_ref.at[d], v_sems.at[d])

    def put_mine(d):
        return pltpu.make_async_copy(mine_ref.at[d], mine_hbm.at[d], mine_sems.at[d])

    def put_other(d):
        return pltpu.make_async_copy(other_ref.at[d], other_hbm.at[d], other_sems.at[d])

    for k in range(chunks):
        fetch_t(k).start()
    for d in range(ahead // 2):
        fetch_v(d).start()
    for k in range(chunks):
        fetch_t(k).wait()
        for s in range(k * each, (k + 1) * each):
            ends = jnp.where(row < part - whole, t_ref[s, whole:, :], 0.0)
            pad = jnp.zeros((PITCH - PADDED, wide), jnp.float32)
            value = jnp.concatenate([t_ref[s, :whole, :], ends, pad], axis=0)
            high = value.astype(jnp.bfloat16)
            high_ref[s] = high
            low_ref[s] = (value - high.astype(jnp.float32)).astype(jnp.bfloat16)

    for d in range(ahead // 2, ahead):
        fetch_v(d).start()
    is_first = core_ref[0] == 0

    def block(d, _):
        @pl.when(d + ahead < cell)
        def _():
            fetch_v(d + ahead).start()

        fetch_v(d).wait()
        total = contract(d)
        mine_ref[d] = jnp.where(is_first, total[:, :LANES], total[:, LANES:])
        other_ref[d] = jnp.where(is_first, total[:, LANES:], total[:, :LANES])
        put_mine(d).start()
        put_other(d).start()
        return 0

    def contract(d):
        def load(q):
            return v_ref[d, :, q * LANES : (q + 1) * LANES]

        def piece(h):
            q, o = divmod(part * h, LANES)
            base = PITCH * (h % 2)
            shift = (base - o) % LANES
            first = pltpu.roll(load(q), shift, 1) if shift else load(q)
            if o + part <= LANES:
                return first
            second = pltpu.roll(load(q + 1), shift, 1) if shift else load(q + 1)
            return jnp.where(lane < base + LANES - o, first, second)

        total = jnp.zeros((4 * rows, wide), jnp.float32)
        minor = jnp.zeros((2 * rows, wide), jnp.float32)
        for g in range(0, tiles, step):
            both = []
            for h in range(g, g + step, 2):
                value = jnp.where(lane < PITCH, piece(h), piece(h + 1))
                zeroth = value * (1.0 - jnp.where(lane_row < PITCH, ids_ref[d, tiles + h], ids_ref[d, tiles + h + 1]))
                value = jnp.concatenate([zeroth, value - zeroth], axis=0)
                rest = value - value.astype(jnp.bfloat16).astype(jnp.float32)
                both.append(jnp.concatenate([value, rest], axis=0).astype(jnp.bfloat16))
            both = jnp.concatenate(both, axis=1)
            at = [ids_ref[d, h].astype(jnp.int32) for h in range(g, g + step)]
            t_high = jnp.concatenate([high_ref[s] for s in at], axis=0)
            t_low = jnp.concatenate([low_ref[s] for s in at], axis=0)
            total += jnp.dot(both, t_high, preferred_element_type=jnp.float32)
            minor += jnp.dot(both[: 2 * rows], t_low, preferred_element_type=jnp.float32)
        return total[: 2 * rows] + total[2 * rows :] + minor

    lax.fori_loop(0, cell, block, 0)
    for d in range(cell):
        put_mine(d).wait()
        put_other(d).wait()


def ladder(ids, core, got, held, part, step):
    cell, rows, width = got.shape
    peers, padded, wide = held.shape
    chunks = 8
    anywhere = pl.BlockSpec(memory_space=pl.ANY)
    scalars = pl.BlockSpec(memory_space=pltpu.SMEM)
    shape = jax.ShapeDtypeStruct((cell, RD * rows, LANES), jnp.float32)
    return pl.pallas_call(
        functools.partial(ladder_kernel, part, step),
        in_specs=[scalars, scalars, anywhere, anywhere],
        out_specs=[anywhere, anywhere],
        out_shape=(shape, shape),
        scratch_shapes=[
            pltpu.VMEM((cell, rows, width), jnp.float32),
            pltpu.VMEM((peers, padded, wide), jnp.float32),
            pltpu.VMEM((peers, PITCH, wide), jnp.bfloat16),
            pltpu.VMEM((peers, PITCH, wide), jnp.bfloat16),
            pltpu.VMEM(shape.shape, jnp.float32),
            pltpu.VMEM(shape.shape, jnp.float32),
            pltpu.SemaphoreType.DMA((chunks,)),
            pltpu.SemaphoreType.DMA((cell,)),
            pltpu.SemaphoreType.DMA((cell,)),
            pltpu.SemaphoreType.DMA((cell,)),
        ],
        compiler_params=pltpu.CompilerParams(vmem_limit_bytes=VMEM),
        cost_estimate=pl.CostEstimate(
            flops=12 * rows * got.size // rows * PITCH // part * wide * RD, bytes_accessed=4 * (got.size + held.size), transcendentals=0
        ),
    )(ids, core, got, held)


def exchange(value, axes):
    return lax.all_to_all(value, axes, split_axis=0, concat_axis=0, tiled=True)


def body(amplitudes, integrals, tile_map, cd_ids, res_ids):
    cell = lax.axis_size(PLANE)
    tiles, rows, depth = integrals.shape
    wide = amplitudes.shape[1]
    part = depth // cell
    peers = tile_map.shape[0]
    shape = tuple(lax.axis_size(a) for a in TILE)
    own = exchange(pack(tile_map, cd_ids, res_ids, amplitudes[0].T, cell, shape), PLANE)
    sent = cut(integrals, cell)
    ids = own[:, part, : 2 * tiles]
    own, sent = lax.optimization_barrier((own, sent))
    shared = lax.all_gather(own, "z").reshape(peers, PADDED, wide)
    sent, ids, core = lax.optimization_barrier((sent, ids, lax.axis_index("slab")))
    got = exchange(sent, PLANE)
    got, shared, ids, core = lax.optimization_barrier((got, shared, ids, core))
    mine, other = ladder(ids, core[None], got, shared, part, 16)
    mine += lax.ppermute(other, "slab", [(0, 1), (1, 0)])
    back = exchange(mine, PLANE)
    return jnp.sum(back, axis=0).reshape(RD, rows, LANES)


def solution(mesh):
    grid = Mesh(mesh.devices.reshape(4, 8, 4, 2), TILE + ("slab",))
    placed = (P(TILE, None, "slab"), P(TILE, None, "slab"), P(), P(TILE), P(TILE))
    return jax.shard_map(
        body, mesh=grid, in_specs=placed, out_specs=P(TILE, None, "slab"), check_vma=False
    )
```

time: 519 us -> 181 us (0.35)
  local copies, waits for them, and re-layouts: 240 us -> 2.36 us
  blocking collectives: 181 us -> 113 us
  matrix products: 56 us -> 0 us
  Pallas kernels: 0 us -> 33.3 us
  other arithmetic: 18.3 us -> 1.81 us
  starting transfers between devices: 4.88 us -> 11.3 us
    all_gather x1 -> x0, blocking collectives: 128 us -> none  [body(): meta = lax.all_gather(jnp.stack([owner, res_ids]), PLANE)]
    reshape x19 -> x0, local copies, waits for them, and re-layouts: 93.6 us -> none  [the longest x16 46.4 us: one(): picked = held[own_rows].reshape(tiles * part, wide)]
    gather x16 -> x0, local copies, waits for them, and re-layouts: 90.6 us -> none  [one(): picked = held[own_rows].reshape(tiles * part, wide)]
    all_to_all x2, blocking collectives: 53 us -> 113 us  [exchange(): return lax.all_to_all(value, axes, split_axis=0, concat_axis=0, tiled=True)]
    dot_general x16 -> x0, matrix products: 56 us -> none  [one(): return jnp.dot(masked, picked, precision=lax.Precision.HIGHEST)]
    pallas_call x0 -> x3, Pallas kernels: none -> 33.3 us  [the longest x1 19.6 us: ladder(): pl.pallas_call(functools.partial(ladder_kernel, part, step), in_specs=[sc...]
    transpose x1 -> x0, local copies, waits for them, and re-layouts: 21.4 us -> none  [body(): integrals.reshape(tiles, rows, cell, part).transpose(2, 1, 0, 3)]
    broadcast_in_dim x48 -> x0, local copies, waits for them, and re-layouts: 21 us -> none  [the longest x32 19.7 us: one(): jnp.where(select[:, None, :], block_v[None], 0.0)]
  transfers between devices with their start and end apart: 2 -> 3, of which waited for: 0 -> 2; matrix products, arithmetic and copies ran while one was open for 15% -> 1% of each run, Pallas kernels for 0% -> 6%
where the time goes in v6:
time: 181 us; the launch traced here: 180 us
  blocking collectives  113 us (62%)
  Pallas kernels  33.3 us (18%)
  between operations  13.4 us (7%)
  starting transfers between devices  11.3 us (6%)
  waiting for transfers between devices  4.94 us (3%)
  local copies, waits for them, and re-layouts  2.36 us (1%)
  other arithmetic  1.81 us (1%)
    all_to_all x2, blocking collectives, exchange(): return lax.all_to_all(value, axes, split_axis=0, concat_axis=0, tiled=True)  113 us
    pallas_call x1, Pallas kernels, ladder(): pl.pallas_call(functools.partial(ladder_kernel, part, step), in_specs=[sc...  19.6 us
    pallas_call x1, Pallas kernels, cut(): pl.pallas_call(functools.partial(cut_kernel, part), grid=(rows // 8,), in...  11.5 us
    all_to_all x1, starting transfers between devices, exchange(): return lax.all_to_all(value, axes, split_axis=0, concat_axis=0, tiled=True)  7.58 us
    ppermute x1, starting transfers between devices, body(): mine += lax.ppermute(other, 'slab', [(0, 1), (1, 0)])  3.71 us
  transfers between devices with their start and end apart: 3, of which 2 were waited for; matrix products, arithmetic and copies ran while one was open for 1% of the time, Pallas kernels for 6%

profile of v6, /device:TPU:1, one launch (start us, length us, event | category | flops | bytes accessed | tf_op | source)
XLA Modules:
  0.0 180.2 jit_solution(13902443151499859762)
XLA Ops:
  6.5 2.2 %shard_map.55 = f32[16,56,256]{2,1,0:T(8,128)} custom-call(s32[1,128]{1,0:T(1,128)} %bitcast.13, s32[1,64]{1,0:T(1,128)} %bitcast.14, s32[1,64]{1,0:T(1,128)} %bitcast.15, f32[800,256]{1,0:T(8,128)} %bitcast.11), custom_call_target="tpu_custom_call" | custom-call | bytes 1638400 | tf_op jit(solution)/shard_map/pallas_call | solution.py:40
  8.8 7.6 %all-to-all-start = ((f32[16,56,256]{2,1,0:T(8,128)}), f32[16,56,256]{2,1,0:T(8,128)S(1)}, u32[]{:S(2)}, u32[]{:S(2)}) async-start(f32[16,56,256]{2,1,0:T(8,128)} %shard_map.55), calls=%async_computation | async-start | bytes 1835008 | tf_op jit(solution)/shard_map/all_to_all | solution.py:220
  16.4 0.0 all-gather.3.cloned.1.call-start
  16.4 11.5 %shard_map.56 = f32[16,40,3200]{2,1,0:T(8,128)} custom-call(f32[64,40,800]{2,1,0:T(8,128)} %v_ref.1), custom_call_target="tpu_custom_call" | custom-call | bytes 16384000 | tf_op jit(solution)/shard_map/pallas_call | solution.py:80
  28.0 3.0 %all-to-all-done = f32[16,56,256]{2,1,0:T(8,128)S(1)} async-done(((f32[16,56,256]{2,1,0:T(8,128)}), f32[16,56,256]{2,1,0:T(8,128)S(1)}, u32[]{:S(2)}, u32[]{:S(2)}) %all-to-all-start) | async-done | bytes 917536 | tf_op jit(solution)/shard_map/all_to_all | solution.py:220
  31.0 0.0 copy-start
  31.0 0.9 copy-done
  31.9 0.0 all-gather.3.cloned.1.call-update
  31.9 1.4 slice.4
  33.4 97.4 %all_to_all.15.v_hbm = f32[16,40,3200]{2,1,0:T(8,128)} all-to-all(f32[16,40,3200]{2,1,0:T(8,128)} %shard_map.56), channel_id=1, replica_groups=mesh['y'=4,'z'=8,'x'=4,'slab'=2] {'y','x'}, dimensions={0} | all-to-all | bytes 16384000 | tf_op jit(solution)/shard_map/all_to_all | solution.py:220
  130.8 0.0 all-gather.3.cloned.1.call-done.t_hbm
  130.8 19.6 %shard_map.57 = (f32[16,80,128]{2,1,0:T(8,128)}, f32[16,80,128]{2,1,0:T(8,128)}) custom-call(f32[16,128]{1,0:T(8,128)} %bitcast.12, s32[1]{0:T(128)} %bitcast.6.core_ref, f32[16,40,3200]{2,1,0:T(8,128)} %all_to_all.15.v_hbm, f32[128,56,256]{2,1,0:T(8,128)} %all-gather.3.cloned.1.call-done.t_hbm), custom_call_target="tpu_custom_call" | custom-call | flops 16106127360 | bytes 15532032 | tf_op jit(solution)/shard_map/pallas_call | solution.py:195
  150.3 3.7 %collective-permute-start = (f32[16,80,128]{2,1,0:T(8,128)}, f32[16,80,128]{2,1,0:T(8,128)S(1)}, u32[]{:S(2)}, u32[]{:S(2)}) collective-permute-start(f32[16,80,128]{2,1,0:T(8,128)} %get-tuple-element.26), channel_id=1, source_target_pairs={{0,1},{1,0},{2,3},{3,2},{4,5},{5,4},{6,7},{7,6},{8,9},{9,8},{10,11... | collective-permute-start | bytes 1966088 | tf_op jit(solution)/shard_map/ppermute | solution.py:239
  154.0 1.9 %collective-permute-done = f32[16,80,128]{2,1,0:T(8,128)S(1)} collective-permute-done((f32[16,80,128]{2,1,0:T(8,128)}, f32[16,80,128]{2,1,0:T(8,128)S(1)}, u32[]{:S(2)}, u32[]{:S(2)}) %collective-permute-start) | collective-permute-done | bytes 655392 | tf_op jit(solution)/shard_map/ppermute | solution.py:239
  156.0 1.2 add.3
  157.1 15.5 %all_to_all.16 = f32[16,80,128]{2,1,0:T(8,128)S(1)} all-to-all(f32[16,80,128]{2,1,0:T(8,128)S(1)} %add.3), channel_id=1, replica_groups=mesh['y'=4,'z'=8,'x'=4,'slab'=2] {'y','x'}, dimensions={0} | all-to-all | bytes 1310720 | tf_op jit(solution)/shard_map/all_to_all | solution.py:220
  172.7 0.7 reduce_sum.9
Async XLA Ops:
  8.8 22.2 %all-to-all-start = ((f32[16,56,256]{2,1,0:T(8,128)}), f32[16,56,256]{2,1,0:T(8,128)S(1)}, u32[]{:S(2)}, u32[]{:S(2)}) async-start(f32[16,56,256]{2,1,0:T(8,128)} %shard_map.55), calls=%async_computation | async-start | bytes 1835008 | tf_op jit(solution)/shard_map/all_to_all | solution.py:220
  16.4 114.4 %all-gather.3.cloned.1.call-start = ((), (), s32[]{:S(2)}) async-start(), calls=%async_computation.3 | async-start | bytes 8257536 | tf_op jit(solution)/shard_map/all_gather | solution.py:234
  31.0 0.9 copy-start
  150.3 5.6 %collective-permute-start = (f32[16,80,128]{2,1,0:T(8,128)}, f32[16,80,128]{2,1,0:T(8,128)S(1)}, u32[]{:S(2)}, u32[]{:S(2)}) collective-permute-start(f32[16,80,128]{2,1,0:T(8,128)} %get-tuple-element.26), channel_id=1, source_target_pairs={{0,1},{1,0},{2,3},{3,2},{4,5},{5,4},{6,7},{7,6},{8,9},{9,8},{10,11... | collective-permute-start | bytes 1966088 | tf_op jit(solution)/shard_map/ppermute | solution.py:239
Sparse Core Ops, SparseCore 0:
  32.0 84.7 all-gather.2

commit v7 on v6

--- a/solution.py
+++ b/solution.py
@@ -16,8 +16,22 @@
 VMEM = 56 * 1024 * 1024
 
 
-def pack_kernel(part, tiles, shape, map_ref, cd_ref, res_ref, t_ref, out_ref):
+def pack_kernel(part, tiles, shape, map_ref, cd_ref, res_ref, t_hbm, out_hbm, t_ref, out_ref, in_sems, out_sems):
     size_y, size_z, size_x = shape
+    cells = out_ref.shape[0]
+    pieces = in_sems.shape[0]
+    each = cells // pieces
+
+    def fetch(k):
+        at = pl.ds(k * each * part, each * part)
+        return pltpu.make_async_copy(t_hbm.at[at], t_ref.at[at], in_sems.at[k])
+
+    def put(k):
+        at = pl.ds(k * each, each)
+        return pltpu.make_async_copy(out_ref.at[at], out_hbm.at[at], out_sems.at[k])
+
+    for k in range(pieces):
+        fetch(k).start()
     square = (LANES, LANES)
     row = lax.broadcasted_iota(jnp.int32, square, 0)
     at_x, at_z, at_y = row % size_x, row // size_x % size_z, row // (size_x * size_z)
@@ -27,19 +41,35 @@
     owner = jnp.sum(jnp.where(match, slot[:, :tiles], 0.0), axis=0, keepdims=True)
     ids = jnp.concatenate([owner, res_ref[...].astype(jnp.float32)], axis=1)
     tail = jnp.zeros((PADDED - part, t_ref.shape[1]), jnp.float32)
-    for c in range(out_ref.shape[0]):
-        out_ref[c, :part, :] = t_ref[c * part : (c + 1) * part, :]
-        out_ref[c, part:, :] = tail
-        out_ref[c, part : part + 1, : 2 * tiles] = ids
+    for k in range(pieces):
+        fetch(k).wait()
+        for c in range(k * each, (k + 1) * each):
+            out_ref[c, :part, :] = t_ref[c * part : (c + 1) * part, :]
+            out_ref[c, part:, :] = tail
+            out_ref[c, part : part + 1, : 2 * tiles] = ids
+        put(k).start()
+    for k in range(pieces):
+        put(k).wait()
 
 
 def pack(tile_map, cd_ids, res_ids, turned, cell, shape):
     depth, wide = turned.shape
     part = depth // cell
     tiles = cd_ids.shape[0]
+    pieces = 4
+    small = pl.BlockSpec(memory_space=pltpu.VMEM)
+    anywhere = pl.BlockSpec(memory_space=pl.ANY)
     return pl.pallas_call(
         functools.partial(pack_kernel, part, tiles, shape),
+        in_specs=[small, small, small, anywhere],
+        out_specs=anywhere,
         out_shape=jax.ShapeDtypeStruct((cell, PADDED, wide), jnp.float32),
+        scratch_shapes=[
+            pltpu.VMEM((depth, wide), jnp.float32),
+            pltpu.VMEM((cell, PADDED, wide), jnp.float32),
+            pltpu.SemaphoreType.DMA((pieces,)),
+            pltpu.SemaphoreType.DMA((pieces,)),
+        ],
         compiler_params=pltpu.CompilerParams(vmem_limit_bytes=VMEM),
         cost_estimate=pl.CostEstimate(flops=0, bytes_accessed=depth * wide * 8, transcendentals=0),
     )(tile_map[None], cd_ids[None], res_ids[None], turned)
@@ -89,8 +119,8 @@
 
 
 def ladder_kernel(
-    part, step, ids_ref, core_ref, v_hbm, t_hbm, mine_hbm, other_hbm,
-    v_ref, t_ref, high_ref, low_ref, mine_ref, other_ref, t_sems, v_sems, mine_sems, other_sems,
+    part, step, at_ref, v_hbm, t_hbm, mine_hbm, other_hbm,
+    v_ref, t_ref, high_ref, low_ref, mine_ref, other_ref, ids_ref, t_sems, v_sems, mine_sems, other_sems, ids_sem,
 ):
     peers, _, wide = t_ref.shape
     cell, rows, _ = v_ref.shape
@@ -116,6 +146,13 @@
     def put_other(d):
         return pltpu.make_async_copy(other_ref.at[d], other_hbm.at[d], other_sems.at[d])
 
+    def own(d, i):
+        return ids_ref[d, part - whole, i]
+
+    fetch_ids = pltpu.make_async_copy(
+        t_hbm.at[pl.ds(at_ref[1] * cell, cell), pl.ds(whole, 8), pl.ds(0, LANES)], ids_ref, ids_sem
+    )
+    fetch_ids.start()
     for k in range(chunks):
         fetch_t(k).start()
     for d in range(ahead // 2):
@@ -132,7 +169,8 @@
 
     for d in range(ahead // 2, ahead):
         fetch_v(d).start()
-    is_first = core_ref[0] == 0
+    fetch_ids.wait()
+    is_first = at_ref[0] == 0
 
     def block(d, _):
         @pl.when(d + ahead < cell)
@@ -167,12 +205,12 @@
             both = []
             for h in range(g, g + step, 2):
                 value = jnp.where(lane < PITCH, piece(h), piece(h + 1))
-                zeroth = value * (1.0 - jnp.where(lane_row < PITCH, ids_ref[d, tiles + h], ids_ref[d, tiles + h + 1]))
+                zeroth = value * (1.0 - jnp.where(lane_row < PITCH, own(d, tiles + h), own(d, tiles + h + 1)))
                 value = jnp.concatenate([zeroth, value - zeroth], axis=0)
                 rest = value - value.astype(jnp.bfloat16).astype(jnp.float32)
                 both.append(jnp.concatenate([value, rest], axis=0).astype(jnp.bfloat16))
             both = jnp.concatenate(both, axis=1)
-            at = [ids_ref[d, h].astype(jnp.int32) for h in range(g, g + step)]
+            at = [own(d, h).astype(jnp.int32) for h in range(g, g + step)]
             t_high = jnp.concatenate([high_ref[s] for s in at], axis=0)
             t_low = jnp.concatenate([low_ref[s] for s in at], axis=0)
             total += jnp.dot(both, t_high, preferred_element_type=jnp.float32)
@@ -185,16 +223,15 @@
         put_other(d).wait()
 
 
-def ladder(ids, core, got, held, part, step):
+def ladder(at, got, held, part, step):
     cell, rows, width = got.shape
     peers, padded, wide = held.shape
     chunks = 8
     anywhere = pl.BlockSpec(memory_space=pl.ANY)
-    scalars = pl.BlockSpec(memory_space=pltpu.SMEM)
     shape = jax.ShapeDtypeStruct((cell, RD * rows, LANES), jnp.float32)
     return pl.pallas_call(
         functools.partial(ladder_kernel, part, step),
-        in_specs=[scalars, scalars, anywhere, anywhere],
+        in_specs=[pl.BlockSpec(memory_space=pltpu.SMEM), anywhere, anywhere],
         out_specs=[anywhere, anywhere],
         out_shape=(shape, shape),
         scratch_shapes=[
@@ -204,16 +241,18 @@
             pltpu.VMEM((peers, PITCH, wide), jnp.bfloat16),
             pltpu.VMEM(shape.shape, jnp.float32),
             pltpu.VMEM(shape.shape, jnp.float32),
+            pltpu.SMEM((cell, 8, LANES), jnp.float32),
             pltpu.SemaphoreType.DMA((chunks,)),
             pltpu.SemaphoreType.DMA((cell,)),
             pltpu.SemaphoreType.DMA((cell,)),
             pltpu.SemaphoreType.DMA((cell,)),
+            pltpu.SemaphoreType.DMA,
         ],
         compiler_params=pltpu.CompilerParams(vmem_limit_bytes=VMEM),
         cost_estimate=pl.CostEstimate(
             flops=12 * rows * got.size // rows * PITCH // part * wide * RD, bytes_accessed=4 * (got.size + held.size), transcendentals=0
         ),
-    )(ids, core, got, held)
+    )(at, got, held)
 
 
 def exchange(value, axes):
@@ -229,13 +268,13 @@
     shape = tuple(lax.axis_size(a) for a in TILE)
     own = exchange(pack(tile_map, cd_ids, res_ids, amplitudes[0].T, cell, shape), PLANE)
     sent = cut(integrals, cell)
-    ids = own[:, part, : 2 * tiles]
     own, sent = lax.optimization_barrier((own, sent))
     shared = lax.all_gather(own, "z").reshape(peers, PADDED, wide)
-    sent, ids, core = lax.optimization_barrier((sent, ids, lax.axis_index("slab")))
+    at = jnp.stack([lax.axis_index("slab"), lax.axis_index("z")])
+    sent, at = lax.optimization_barrier((sent, at))
     got = exchange(sent, PLANE)
-    got, shared, ids, core = lax.optimization_barrier((got, shared, ids, core))
-    mine, other = ladder(ids, core[None], got, shared, part, 16)
+    got, shared, at = lax.optimization_barrier((got, shared, at))
+    mine, other = ladder(at, got, shared, part, 16)
     mine += lax.ppermute(other, "slab", [(0, 1), (1, 0)])
     back = exchange(mine, PLANE)
     return jnp.sum(back, axis=0).reshape(RD, rows, LANES)

time: 181 us -> 180 us (level)
  transfers between devices with their start and end apart: 3 -> 3, of which waited for: 2 -> 2; matrix products, arithmetic and copies ran while one was open for 1% -> 0% of each run, Pallas kernels for 6% -> 6%
where the time goes in v7:
time: 180 us
  blocking collectives  113 us (63%)
  Pallas kernels  33.7 us (19%)
  between operations  13.4 us (7%)
  starting transfers between devices  11.3 us (6%)
  waiting for transfers between devices  4.86 us (3%)
  other arithmetic  2.46 us (1%)
    all_to_all x2, blocking collectives, exchange(): return lax.all_to_all(value, axes, split_axis=0, concat_axis=0, tiled=True)  113 us
    pallas_call x1, Pallas kernels, ladder(): pl.pallas_call(functools.partial(ladder_kernel, part, step), in_specs=[pl...  19.4 us
    pallas_call x1, Pallas kernels, cut(): pl.pallas_call(functools.partial(cut_kernel, part), grid=(rows // 8,), in...  11.6 us
    all_to_all x1, starting transfers between devices, exchange(): return lax.all_to_all(value, axes, split_axis=0, concat_axis=0, tiled=True)  7.6 us
    ppermute x1, starting transfers between devices, body(): mine += lax.ppermute(other, 'slab', [(0, 1), (1, 0)])  3.7 us
  transfers between devices with their start and end apart: 3, of which 2 were waited for; matrix products, arithmetic and copies ran while one was open for 0% of the time, Pallas kernels for 6%

profile of v7, /device:TPU:1, one launch (start us, length us, event | category | flops | bytes accessed | tf_op | source)
XLA Modules:
  0.0 179.8 jit_solution(15319309311444607314)
XLA Ops:
  6.5 2.7 %shard_map.55 = f32[16,56,256]{2,1,0:T(8,128)} custom-call(s32[1,128]{1,0:T(1,128)} %bitcast.10, s32[1,64]{1,0:T(1,128)} %bitcast.11, s32[1,64]{1,0:T(1,128)} %bitcast.12, f32[800,256]{1,0:T(8,128)} %bitcast.9), custom_call_target="tpu_custom_call" | custom-call | bytes 1638400 | tf_op jit(solution)/shard_map/pallas_call | solution.py:62
  9.3 7.6 %all-to-all-start = ((f32[16,56,256]{2,1,0:T(8,128)}), f32[16,56,256]{2,1,0:T(8,128)S(1)}, u32[]{:S(2)}, u32[]{:S(2)}) async-start(f32[16,56,256]{2,1,0:T(8,128)} %shard_map.55), calls=%async_computation | async-start | bytes 1835008 | tf_op jit(solution)/shard_map/all_to_all | solution.py:259
  16.9 0.0 all-gather.3.cloned.1.call-start
  16.9 11.6 %shard_map.56 = f32[16,40,3200]{2,1,0:T(8,128)} custom-call(f32[64,40,800]{2,1,0:T(8,128)} %v_ref.1), custom_call_target="tpu_custom_call" | custom-call | bytes 16384000 | tf_op jit(solution)/shard_map/pallas_call | solution.py:110
  28.5 2.9 %all-to-all-done = f32[16,56,256]{2,1,0:T(8,128)S(1)} async-done(((f32[16,56,256]{2,1,0:T(8,128)}), f32[16,56,256]{2,1,0:T(8,128)S(1)}, u32[]{:S(2)}, u32[]{:S(2)}) %all-to-all-start) | async-done | bytes 917536 | tf_op jit(solution)/shard_map/all_to_all | solution.py:259
  31.4 0.0 copy-start
  31.4 0.9 copy-done
  32.4 0.0 all-gather.3.cloned.1.call-update
  32.4 0.6 pad_add_fusion.at_ref
  33.0 97.5 %all_to_all.15.v_hbm = f32[16,40,3200]{2,1,0:T(8,128)} all-to-all(f32[16,40,3200]{2,1,0:T(8,128)} %shard_map.56), channel_id=1, replica_groups=mesh['y'=4,'z'=8,'x'=4,'slab'=2] {'y','x'}, dimensions={0} | all-to-all | bytes 16384000 | tf_op jit(solution)/shard_map/all_to_all | solution.py:259
  130.5 0.0 all-gather.3.cloned.1.call-done.t_hbm
  130.5 19.4 %shard_map.57 = (f32[16,80,128]{2,1,0:T(8,128)}, f32[16,80,128]{2,1,0:T(8,128)}) custom-call(s32[2]{0:T(128)} %pad_add_fusion.at_ref, f32[16,40,3200]{2,1,0:T(8,128)} %all_to_all.15.v_hbm, f32[128,56,256]{2,1,0:T(8,128)} %all-gather.3.cloned.1.call-done.t_hbm), custom_call_target="tpu_custom_call" | custom-call | flops 16106127360 | bytes 15532032 | tf_op jit(solution)/shard_map/pallas_call | solution.py:232
  149.9 3.7 %collective-permute-start = (f32[16,80,128]{2,1,0:T(8,128)}, f32[16,80,128]{2,1,0:T(8,128)S(1)}, u32[]{:S(2)}, u32[]{:S(2)}) collective-permute-start(f32[16,80,128]{2,1,0:T(8,128)} %get-tuple-element.22), channel_id=1, source_target_pairs={{0,1},{1,0},{2,3},{3,2},{4,5},{5,4},{6,7},{7,6},{8,9},{9,8},{10,11... | collective-permute-start | bytes 1966088 | tf_op jit(solution)/shard_map/ppermute | solution.py:278
  153.6 1.9 %collective-permute-done = f32[16,80,128]{2,1,0:T(8,128)S(1)} collective-permute-done((f32[16,80,128]{2,1,0:T(8,128)}, f32[16,80,128]{2,1,0:T(8,128)S(1)}, u32[]{:S(2)}, u32[]{:S(2)}) %collective-permute-start) | collective-permute-done | bytes 655392 | tf_op jit(solution)/shard_map/ppermute | solution.py:278
  155.6 1.2 add.3
  156.7 15.5 %all_to_all.16 = f32[16,80,128]{2,1,0:T(8,128)S(1)} all-to-all(f32[16,80,128]{2,1,0:T(8,128)S(1)} %add.3), channel_id=1, replica_groups=mesh['y'=4,'z'=8,'x'=4,'slab'=2] {'y','x'}, dimensions={0} | all-to-all | bytes 1310720 | tf_op jit(solution)/shard_map/all_to_all | solution.py:259
  172.3 0.7 reduce_sum.9
Async XLA Ops:
  9.3 22.2 %all-to-all-start = ((f32[16,56,256]{2,1,0:T(8,128)}), f32[16,56,256]{2,1,0:T(8,128)S(1)}, u32[]{:S(2)}, u32[]{:S(2)}) async-start(f32[16,56,256]{2,1,0:T(8,128)} %shard_map.55), calls=%async_computation | async-start | bytes 1835008 | tf_op jit(solution)/shard_map/all_to_all | solution.py:259
  16.9 113.7 %all-gather.3.cloned.1.call-start = ((), (), s32[]{:S(2)}) async-start(), calls=%async_computation.3 | async-start | bytes 8257536 | tf_op jit(solution)/shard_map/all_gather | solution.py:272
  31.4 0.9 copy-start
  149.9 5.6 %collective-permute-start = (f32[16,80,128]{2,1,0:T(8,128)}, f32[16,80,128]{2,1,0:T(8,128)S(1)}, u32[]{:S(2)}, u32[]{:S(2)}) collective-permute-start(f32[16,80,128]{2,1,0:T(8,128)} %get-tuple-element.22), channel_id=1, source_target_pairs={{0,1},{1,0},{2,3},{3,2},{4,5},{5,4},{6,7},{7,6},{8,9},{9,8},{10,11... | collective-permute-start | bytes 1966088 | tf_op jit(solution)/shard_map/ppermute | solution.py:278
Sparse Core Ops, SparseCore 0:
  32.5 84.8 all-gather.2

commit v8 on v6

--- a/solution.py
+++ b/solution.py
@@ -14,6 +14,7 @@
 PITCH = 64
 PADDED = 56
 VMEM = 56 * 1024 * 1024
+CUT_VMEM = (64 * 1024 - 512) * 1024
 
 
 def pack_kernel(part, tiles, shape, map_ref, cd_ref, res_ref, t_ref, out_ref):
@@ -83,14 +84,14 @@
         in_specs=[pl.BlockSpec((tiles, 8, depth), lambda i: (0, i, 0))],
         out_specs=pl.BlockSpec((cells, 8, tiles * part), lambda i: (0, i, 0)),
         out_shape=jax.ShapeDtypeStruct((cells, rows, tiles * part), jnp.float32),
-        compiler_params=pltpu.CompilerParams(vmem_limit_bytes=VMEM),
+        compiler_params=pltpu.CompilerParams(vmem_limit_bytes=CUT_VMEM),
         cost_estimate=pl.CostEstimate(flops=0, bytes_accessed=tiles * rows * depth * 8, transcendentals=0),
     )(integrals)
 
 
 def ladder_kernel(
-    part, step, ids_ref, core_ref, v_hbm, t_hbm, mine_hbm, other_hbm,
-    v_ref, t_ref, high_ref, low_ref, mine_ref, other_ref, t_sems, v_sems, mine_sems, other_sems,
+    part, step, core_ref, plane_ref, v_hbm, t_hbm, mine_hbm, other_hbm,
+    v_ref, t_ref, high_ref, low_ref, mine_ref, other_ref, ids_ref, t_sems, v_sems, mine_sems, other_sems, ids_sem,
 ):
     peers, _, wide = t_ref.shape
     cell, rows, _ = v_ref.shape
@@ -116,6 +117,13 @@
     def put_other(d):
         return pltpu.make_async_copy(other_ref.at[d], other_hbm.at[d], other_sems.at[d])
 
+    def own(d, i):
+        return ids_ref[d, part - whole, i]
+
+    fetch_ids = pltpu.make_async_copy(
+        t_hbm.at[pl.ds(plane_ref[0] * cell, cell), pl.ds(whole, 8), pl.ds(0, LANES)], ids_ref, ids_sem
+    )
+    fetch_ids.start()
     for k in range(chunks):
         fetch_t(k).start()
     for d in range(ahead // 2):
@@ -132,6 +140,7 @@
 
     for d in range(ahead // 2, ahead):
         fetch_v(d).start()
+    fetch_ids.wait()
     is_first = core_ref[0] == 0
 
     def block(d, _):
@@ -167,12 +176,12 @@
             both = []
             for h in range(g, g + step, 2):
                 value = jnp.where(lane < PITCH, piece(h), piece(h + 1))
-                zeroth = value * (1.0 - jnp.where(lane_row < PITCH, ids_ref[d, tiles + h], ids_ref[d, tiles + h + 1]))
+                zeroth = value * (1.0 - jnp.where(lane_row < PITCH, own(d, tiles + h), own(d, tiles + h + 1)))
                 value = jnp.concatenate([zeroth, value - zeroth], axis=0)
                 rest = value - value.astype(jnp.bfloat16).astype(jnp.float32)
                 both.append(jnp.concatenate([value, rest], axis=0).astype(jnp.bfloat16))
             both = jnp.concatenate(both, axis=1)
-            at = [ids_ref[d, h].astype(jnp.int32) for h in range(g, g + step)]
+            at = [own(d, h).astype(jnp.int32) for h in range(g, g + step)]
             t_high = jnp.concatenate([high_ref[s] for s in at], axis=0)
             t_low = jnp.concatenate([low_ref[s] for s in at], axis=0)
             total += jnp.dot(both, t_high, preferred_element_type=jnp.float32)
@@ -185,16 +194,16 @@
         put_other(d).wait()
 
 
-def ladder(ids, core, got, held, part, step):
+def ladder(core, plane, got, held, part, step):
     cell, rows, width = got.shape
     peers, padded, wide = held.shape
     chunks = 8
     anywhere = pl.BlockSpec(memory_space=pl.ANY)
-    scalars = pl.BlockSpec(memory_space=pltpu.SMEM)
+    scalar = pl.BlockSpec(memory_space=pltpu.SMEM)
     shape = jax.ShapeDtypeStruct((cell, RD * rows, LANES), jnp.float32)
     return pl.pallas_call(
         functools.partial(ladder_kernel, part, step),
-        in_specs=[scalars, scalars, anywhere, anywhere],
+        in_specs=[scalar, scalar, anywhere, anywhere],
         out_specs=[anywhere, anywhere],
         out_shape=(shape, shape),
         scratch_shapes=[
@@ -204,16 +213,18 @@
             pltpu.VMEM((peers, PITCH, wide), jnp.bfloat16),
             pltpu.VMEM(shape.shape, jnp.float32),
             pltpu.VMEM(shape.shape, jnp.float32),
+            pltpu.SMEM((cell, 8, LANES), jnp.float32),
             pltpu.SemaphoreType.DMA((chunks,)),
             pltpu.SemaphoreType.DMA((cell,)),
             pltpu.SemaphoreType.DMA((cell,)),
             pltpu.SemaphoreType.DMA((cell,)),
+            pltpu.SemaphoreType.DMA,
         ],
         compiler_params=pltpu.CompilerParams(vmem_limit_bytes=VMEM),
         cost_estimate=pl.CostEstimate(
             flops=12 * rows * got.size // rows * PITCH // part * wide * RD, bytes_accessed=4 * (got.size + held.size), transcendentals=0
         ),
-    )(ids, core, got, held)
+    )(core, plane, got, held)
 
 
 def exchange(value, axes):
@@ -229,13 +240,12 @@
     shape = tuple(lax.axis_size(a) for a in TILE)
     own = exchange(pack(tile_map, cd_ids, res_ids, amplitudes[0].T, cell, shape), PLANE)
     sent = cut(integrals, cell)
-    ids = own[:, part, : 2 * tiles]
     own, sent = lax.optimization_barrier((own, sent))
     shared = lax.all_gather(own, "z").reshape(peers, PADDED, wide)
-    sent, ids, core = lax.optimization_barrier((sent, ids, lax.axis_index("slab")))
+    sent, core, plane = lax.optimization_barrier((sent, lax.axis_index("slab"), lax.axis_index("z")))
     got = exchange(sent, PLANE)
-    got, shared, ids, core = lax.optimization_barrier((got, shared, ids, core))
-    mine, other = ladder(ids, core[None], got, shared, part, 16)
+    got, shared, core, plane = lax.optimization_barrier((got, shared, core, plane))
+    mine, other = ladder(core[None], plane[None], got, shared, part, 16)
     mine += lax.ppermute(other, "slab", [(0, 1), (1, 0)])
     back = exchange(mine, PLANE)
     return jnp.sum(back, axis=0).reshape(RD, rows, LANES)

time: 181 us -> 178 us (0.983)
  local copies, waits for them, and re-layouts: 2.36 us -> 0 us
  transfers between devices with their start and end apart: 3 -> 3, of which waited for: 2 -> 2; matrix products, arithmetic and copies ran while one was open for 1% -> 0% of each run, Pallas kernels for 6% -> 6%
where the time goes in v8:
time: 178 us; the launch traced here: 177 us
  blocking collectives  113 us (63%)
  Pallas kernels  32.5 us (18%)
  between operations  13.4 us (8%)
  starting transfers between devices  11.4 us (6%)
  waiting for transfers between devices  5.04 us (3%)
  other arithmetic  1.81 us (1%)
    all_to_all x2, blocking collectives, exchange(): return lax.all_to_all(value, axes, split_axis=0, concat_axis=0, tiled=True)  113 us
    pallas_call x1, Pallas kernels, ladder(): pl.pallas_call(functools.partial(ladder_kernel, part, step), in_specs=[sc...  18.8 us
    pallas_call x1, Pallas kernels, cut(): pl.pallas_call(functools.partial(cut_kernel, part), grid=(rows // 8,), in...  11.5 us
    all_to_all x1, starting transfers between devices, exchange(): return lax.all_to_all(value, axes, split_axis=0, concat_axis=0, tiled=True)  7.63 us
    ppermute x1, starting transfers between devices, body(): mine += lax.ppermute(other, 'slab', [(0, 1), (1, 0)])  3.71 us
  transfers between devices with their start and end apart: 3, of which 2 were waited for; matrix products, arithmetic and copies ran while one was open for 0% of the time, Pallas kernels for 6%

profile of v8, /device:TPU:1, one launch (start us, length us, event | category | flops | bytes accessed | tf_op | source)
XLA Modules:
  0.0 177.1 jit_solution(899484396127797531)
XLA Ops:
  6.5 2.3 %shard_map.55 = f32[16,56,256]{2,1,0:T(8,128)} custom-call(s32[1,128]{1,0:T(1,128)} %bitcast.10, s32[1,64]{1,0:T(1,128)} %bitcast.11, s32[1,64]{1,0:T(1,128)} %bitcast.12, f32[800,256]{1,0:T(8,128)} %bitcast.9), custom_call_target="tpu_custom_call" | custom-call | bytes 1638400 | tf_op jit(solution)/shard_map/pallas_call | solution.py:41
  8.8 7.6 %all-to-all-start = ((f32[16,56,256]{2,1,0:T(8,128)}), f32[16,56,256]{2,1,0:T(8,128)}, u32[]{:S(2)}, u32[]{:S(2)}) async-start(f32[16,56,256]{2,1,0:T(8,128)} %shard_map.55), calls=%async_computation | async-start | bytes 1835008 | tf_op jit(solution)/shard_map/all_to_all | solution.py:231
  16.4 0.0 all-gather.3.cloned.1.call-start
  16.5 11.5 %shard_map.56 = f32[16,40,3200]{2,1,0:T(8,128)} custom-call(f32[64,40,800]{2,1,0:T(8,128)} %v_ref.1), custom_call_target="tpu_custom_call" | custom-call | bytes 16384000 | tf_op jit(solution)/shard_map/pallas_call | solution.py:81
  28.0 3.1 %all-to-all-done = f32[16,56,256]{2,1,0:T(8,128)} async-done(((f32[16,56,256]{2,1,0:T(8,128)}), f32[16,56,256]{2,1,0:T(8,128)}, u32[]{:S(2)}, u32[]{:S(2)}) %all-to-all-start) | async-done | bytes 917536 | tf_op jit(solution)/shard_map/all_to_all | solution.py:231
  31.1 0.0 all-gather.3.cloned.1.call-update
  31.1 97.4 %all_to_all.15.v_hbm = f32[16,40,3200]{2,1,0:T(8,128)} all-to-all(f32[16,40,3200]{2,1,0:T(8,128)} %shard_map.56), channel_id=1, replica_groups=mesh['y'=4,'z'=8,'x'=4,'slab'=2] {'y','x'}, dimensions={0} | all-to-all | bytes 16384000 | tf_op jit(solution)/shard_map/all_to_all | solution.py:231
  128.5 0.0 all-gather.3.cloned.1.call-done.t_hbm
  128.5 18.8 %shard_map.57 = (f32[16,80,128]{2,1,0:T(8,128)}, f32[16,80,128]{2,1,0:T(8,128)}) custom-call(s32[1]{0:T(128)} %bitcast.5.core_ref, s32[1]{0:T(128)} %bitcast.6.plane_ref, f32[16,40,3200]{2,1,0:T(8,128)} %all_to_all.15.v_hbm, f32[128,56,256]{2,1,0:T(8,128)} %all-gather.3.cloned.1.call-done.t_hbm), custom_call_target="tpu_custom_call" | custom-call | flops 16106127360 | bytes 15532032 | tf_op jit(solution)/shard_map/pallas_call | solution.py:204
  147.3 3.7 %collective-permute-start = (f32[16,80,128]{2,1,0:T(8,128)}, f32[16,80,128]{2,1,0:T(8,128)S(1)}, u32[]{:S(2)}, u32[]{:S(2)}) collective-permute-start(f32[16,80,128]{2,1,0:T(8,128)} %get-tuple-element.26), channel_id=1, source_target_pairs={{0,1},{1,0},{2,3},{3,2},{4,5},{5,4},{6,7},{7,6},{8,9},{9,8},{10,11... | collective-permute-start | bytes 1966088 | tf_op jit(solution)/shard_map/ppermute | solution.py:249
  151.0 1.9 %collective-permute-done = f32[16,80,128]{2,1,0:T(8,128)S(1)} collective-permute-done((f32[16,80,128]{2,1,0:T(8,128)}, f32[16,80,128]{2,1,0:T(8,128)S(1)}, u32[]{:S(2)}, u32[]{:S(2)}) %collective-permute-start) | collective-permute-done | bytes 655392 | tf_op jit(solution)/shard_map/ppermute | solution.py:249
  153.0 1.2 add.3
  154.1 15.5 %all_to_all.16 = f32[16,80,128]{2,1,0:T(8,128)S(1)} all-to-all(f32[16,80,128]{2,1,0:T(8,128)S(1)} %add.3), channel_id=1, replica_groups=mesh['y'=4,'z'=8,'x'=4,'slab'=2] {'y','x'}, dimensions={0} | all-to-all | bytes 1310720 | tf_op jit(solution)/shard_map/all_to_all | solution.py:231
  169.6 0.7 reduce_sum.9
Async XLA Ops:
  8.8 22.3 %all-to-all-start = ((f32[16,56,256]{2,1,0:T(8,128)}), f32[16,56,256]{2,1,0:T(8,128)}, u32[]{:S(2)}, u32[]{:S(2)}) async-start(f32[16,56,256]{2,1,0:T(8,128)} %shard_map.55), calls=%async_computation | async-start | bytes 1835008 | tf_op jit(solution)/shard_map/all_to_all | solution.py:231
  16.4 112.1 %all-gather.3.cloned.1.call-start = ((), (), s32[]{:S(2)}) async-start(), calls=%async_computation.3 | async-start | bytes 8257536 | tf_op jit(solution)/shard_map/all_gather | solution.py:244
  147.3 5.6 %collective-permute-start = (f32[16,80,128]{2,1,0:T(8,128)}, f32[16,80,128]{2,1,0:T(8,128)S(1)}, u32[]{:S(2)}, u32[]{:S(2)}) collective-permute-start(f32[16,80,128]{2,1,0:T(8,128)} %get-tuple-element.26), channel_id=1, source_target_pairs={{0,1},{1,0},{2,3},{3,2},{4,5},{5,4},{6,7},{7,6},{8,9},{9,8},{10,11... | collective-permute-start | bytes 1966088 | tf_op jit(solution)/shard_map/ppermute | solution.py:249
Sparse Core Ops, SparseCore 0:
  31.2 84.6 all-gather.2

commit v9 on v8

--- a/solution.py
+++ b/solution.py
@@ -11,7 +11,7 @@
 PLANE = ("y", "x")
 TILE = ("y", "z", "x")
 LANES = 128
-PITCH = 64
+MAIN = 48
 PADDED = 56
 VMEM = 56 * 1024 * 1024
 CUT_VMEM = (64 * 1024 - 512) * 1024
@@ -26,12 +26,20 @@
     ids = jnp.transpose(jnp.broadcast_to(map_ref[...].astype(jnp.float32), square))
     match = ids[:, :tiles] == cd_ref[...].astype(jnp.float32)
     owner = jnp.sum(jnp.where(match, slot[:, :tiles], 0.0), axis=0, keepdims=True)
-    ids = jnp.concatenate([owner, res_ref[...].astype(jnp.float32)], axis=1)
+    target = res_ref[...].astype(jnp.float32)
+    ids = jnp.concatenate([owner, target], axis=1)
+    row, lane = row[:tiles], lax.broadcasted_iota(jnp.int32, (tiles, LANES), 1)
+    pairs = (lane // 2 == row).astype(jnp.float32)
+    down = jnp.transpose(jnp.broadcast_to(ids, square))
+    owners = jnp.sum(pairs * down[:tiles], axis=0, keepdims=True)
+    targets = jnp.sum(pairs * down[tiles:], axis=0, keepdims=True)
     tail = jnp.zeros((PADDED - part, t_ref.shape[1]), jnp.float32)
     for c in range(out_ref.shape[0]):
         out_ref[c, :part, :] = t_ref[c * part : (c + 1) * part, :]
         out_ref[c, part:, :] = tail
         out_ref[c, part : part + 1, : 2 * tiles] = ids
+        out_ref[c, part + 1 : part + 2, :LANES] = owners
+        out_ref[c, part + 2 : part + 3, :LANES] = targets
 
 
 def pack(tile_map, cd_ids, res_ids, turned, cell, shape):
@@ -47,7 +55,7 @@
 
 
 def cut_kernel(part, v_ref, out_ref):
-    depth = v_ref.shape[2]
+    tiles, _, depth = v_ref.shape
     lane = lax.broadcasted_iota(jnp.int32, (8, LANES), 1)
     full = depth // LANES
 
@@ -63,12 +71,14 @@
             made = None
             at = j * LANES
             while at < (j + 1) * LANES:
-                h, v = divmod(at, part)
-                q, o = divmod(c * part + v, LANES)
-                run = min(part - v, LANES - o, (j + 1) * LANES - at)
-                key = (h, q)
+                h, v = divmod(at, MAIN) if at < MAIN * tiles else divmod(at - MAIN * tiles, part - MAIN)
+                length = MAIN if at < MAIN * tiles else part - MAIN
+                left = 0 if at < MAIN * tiles else MAIN
+                q, o = divmod(c * part + left + v, LANES)
+                run = min(length - v, LANES - o, (j + 1) * LANES - at)
+                key = (h, q, left)
                 if key not in rolled:
-                    shift = (part * (h - c)) % LANES
+                    shift = (at - o) % LANES
                     rolled[key] = pltpu.roll(source(h, q), shift, 1) if shift else source(h, q)
                 made = rolled[key] if made is None else jnp.where(lane >= at - j * LANES, rolled[key], made)
                 at += run
@@ -91,7 +101,8 @@
 
 def ladder_kernel(
     part, step, core_ref, plane_ref, v_hbm, t_hbm, mine_hbm, other_hbm,
-    v_ref, t_ref, high_ref, low_ref, mine_ref, other_ref, ids_ref, t_sems, v_sems, mine_sems, other_sems, ids_sem,
+    v_ref, t_ref, high_ref, low_ref, rest_ref, pairs_ref, few_ref, routed_ref, start_ref, mine_ref, other_ref, ids_ref,
+    t_sems, v_sems, mine_sems, other_sems, ids_sem, pairs_sem, few_sem,
 ):
     peers, _, wide = t_ref.shape
     cell, rows, _ = v_ref.shape
@@ -99,10 +110,10 @@
     chunks = t_sems.shape[0]
     ahead = 4
     each = peers // chunks
-    lane = lax.broadcasted_iota(jnp.int32, (rows, LANES), 1)
     lane_row = lax.broadcasted_iota(jnp.int32, (1, LANES), 1)
-    whole = part // 8 * 8
-    row = lax.broadcasted_iota(jnp.int32, (PADDED - whole, wide), 0)
+    few = part - MAIN
+    place = lax.broadcasted_iota(jnp.int32, (LANES, few * peers), 1)
+    which = lax.broadcasted_iota(jnp.int32, (LANES, few * peers), 0) % few
 
     def fetch_t(k):
         at = pl.ds(k * each, each)
@@ -118,26 +129,54 @@
         return pltpu.make_async_copy(other_ref.at[d], other_hbm.at[d], other_sems.at[d])
 
     def own(d, i):
-        return ids_ref[d, part - whole, i]
+        return ids_ref[d, few, i]
 
     fetch_ids = pltpu.make_async_copy(
-        t_hbm.at[pl.ds(plane_ref[0] * cell, cell), pl.ds(whole, 8), pl.ds(0, LANES)], ids_ref, ids_sem
+        t_hbm.at[pl.ds(plane_ref[0] * cell, cell), pl.ds(MAIN, 8), pl.ds(0, LANES)], ids_ref, ids_sem
     )
+    fetch_pairs = pltpu.make_async_copy(
+        t_hbm.at[pl.ds(plane_ref[0] * cell, cell), pl.ds(MAIN, 8), pl.ds(0, LANES)], pairs_ref, pairs_sem
+    )
+    fetch_few = pltpu.make_async_copy(v_hbm.at[:, :, pl.ds(MAIN * tiles, LANES)], few_ref, few_sem)
     fetch_ids.start()
+    fetch_pairs.start()
+    fetch_few.start()
     for k in range(chunks):
         fetch_t(k).start()
     for d in range(ahead // 2):
         fetch_v(d).start()
+    def apart(value, target):
+        zeroth = value * (1.0 - target)
+        value = jnp.concatenate([zeroth, value - zeroth], axis=0)
+        rest = value - value.astype(jnp.bfloat16).astype(jnp.float32)
+        return jnp.concatenate([value, rest], axis=0).astype(jnp.bfloat16)
+
+    fetch_pairs.wait()
+    fetch_few.wait()
+    for d in range(cell):
+        column = jnp.transpose(jnp.broadcast_to(pairs_ref[d, few + 1 : few + 2, :], (LANES, LANES)))
+        column = jnp.concatenate([column] * few, axis=1).astype(jnp.int32)
+        route = (place == column + which * peers).astype(jnp.float32).astype(jnp.bfloat16)
+        both = apart(few_ref[d], pairs_ref[d, few + 2 : few + 3, :])
+        routed_ref[d] = jnp.dot(both, route, preferred_element_type=jnp.float32).astype(jnp.bfloat16)
     for k in range(chunks):
         fetch_t(k).wait()
         for s in range(k * each, (k + 1) * each):
-            ends = jnp.where(row < part - whole, t_ref[s, whole:, :], 0.0)
-            pad = jnp.zeros((PITCH - PADDED, wide), jnp.float32)
-            value = jnp.concatenate([t_ref[s, :whole, :], ends, pad], axis=0)
+            value = t_ref[s, :MAIN, :]
             high = value.astype(jnp.bfloat16)
             high_ref[s] = high
             low_ref[s] = (value - high.astype(jnp.float32)).astype(jnp.bfloat16)
-
+    for e in range(few):
+        value = t_ref[:, MAIN + e, :]
+        high = value.astype(jnp.bfloat16)
+        rest_ref[0, e * peers : (e + 1) * peers, :] = high
+        rest_ref[1, e * peers : (e + 1) * peers, :] = (value - high.astype(jnp.float32)).astype(jnp.bfloat16)
+    start = jnp.dot(routed_ref[...].reshape(cell * 4 * rows, wide), rest_ref[0], preferred_element_type=jnp.float32)
+    start = start.reshape(cell, 4 * rows, wide)
+    start = start[:, : 2 * rows] + start[:, 2 * rows :]
+    minor = routed_ref[:, : 2 * rows, :].reshape(cell * 2 * rows, wide)
+    minor = jnp.dot(minor, rest_ref[1], preferred_element_type=jnp.float32)
+    start_ref[...] = start + minor.reshape(cell, 2 * rows, wide)
     for d in range(ahead // 2, ahead):
         fetch_v(d).start()
     fetch_ids.wait()
@@ -160,27 +199,18 @@
         def load(q):
             return v_ref[d, :, q * LANES : (q + 1) * LANES]
 
-        def piece(h):
-            q, o = divmod(part * h, LANES)
-            base = PITCH * (h % 2)
-            shift = (base - o) % LANES
-            first = pltpu.roll(load(q), shift, 1) if shift else load(q)
-            if o + part <= LANES:
-                return first
-            second = pltpu.roll(load(q + 1), shift, 1) if shift else load(q + 1)
-            return jnp.where(lane < base + LANES - o, first, second)
+        def targets(j):
+            first = j * LANES // MAIN
+            made = own(d, tiles + first)
+            for h in range(first + 1, (j * LANES + LANES - 1) // MAIN + 1):
+                made = jnp.where(lane_row < MAIN * h - j * LANES, made, own(d, tiles + h))
+            return made
 
         total = jnp.zeros((4 * rows, wide), jnp.float32)
-        minor = jnp.zeros((2 * rows, wide), jnp.float32)
+        minor = start_ref[d]
         for g in range(0, tiles, step):
-            both = []
-            for h in range(g, g + step, 2):
-                value = jnp.where(lane < PITCH, piece(h), piece(h + 1))
-                zeroth = value * (1.0 - jnp.where(lane_row < PITCH, own(d, tiles + h), own(d, tiles + h + 1)))
-                value = jnp.concatenate([zeroth, value - zeroth], axis=0)
-                rest = value - value.astype(jnp.bfloat16).astype(jnp.float32)
-                both.append(jnp.concatenate([value, rest], axis=0).astype(jnp.bfloat16))
-            both = jnp.concatenate(both, axis=1)
+            span = range(g * MAIN // LANES, (g + step) * MAIN // LANES)
+            both = jnp.concatenate([apart(load(j), targets(j)) for j in span], axis=1)
             at = [own(d, h).astype(jnp.int32) for h in range(g, g + step)]
             t_high = jnp.concatenate([high_ref[s] for s in at], axis=0)
             t_low = jnp.concatenate([low_ref[s] for s in at], axis=0)
@@ -209,8 +239,13 @@
         scratch_shapes=[
             pltpu.VMEM((cell, rows, width), jnp.float32),
             pltpu.VMEM((peers, padded, wide), jnp.float32),
-            pltpu.VMEM((peers, PITCH, wide), jnp.bfloat16),
-            pltpu.VMEM((peers, PITCH, wide), jnp.bfloat16),
+            pltpu.VMEM((peers, MAIN, wide), jnp.bfloat16),
+            pltpu.VMEM((peers, MAIN, wide), jnp.bfloat16),
+            pltpu.VMEM((2, (part - MAIN) * peers, wide), jnp.bfloat16),
+            pltpu.VMEM((cell, 8, LANES), jnp.float32),
+            pltpu.VMEM((cell, rows, LANES), jnp.float32),
+            pltpu.VMEM((cell, 4 * rows, (part - MAIN) * peers), jnp.bfloat16),
+            pltpu.VMEM((cell, 2 * rows, wide), jnp.float32),
             pltpu.VMEM(shape.shape, jnp.float32),
             pltpu.VMEM(shape.shape, jnp.float32),
             pltpu.SMEM((cell, 8, LANES), jnp.float32),
@@ -219,10 +254,12 @@
             pltpu.SemaphoreType.DMA((cell,)),
             pltpu.SemaphoreType.DMA((cell,)),
             pltpu.SemaphoreType.DMA,
+            pltpu.SemaphoreType.DMA,
+            pltpu.SemaphoreType.DMA,
         ],
         compiler_params=pltpu.CompilerParams(vmem_limit_bytes=VMEM),
         cost_estimate=pl.CostEstimate(
-            flops=12 * rows * got.size // rows * PITCH // part * wide * RD, bytes_accessed=4 * (got.size + held.size), transcendentals=0
+            flops=12 * rows * got.size // rows * wide * RD, bytes_accessed=4 * (got.size + held.size), transcendentals=0
         ),
     )(core, plane, got, held)
 

time: 178 us -> 178 us (level)
  Pallas kernels: 32.5 us -> 36.2 us
  waiting for transfers between devices: 5.04 us -> 1.96 us
  blocking collectives: 113 us -> 115 us
    pallas_call x1, Pallas kernels: 11.5 us -> 15.7 us  [cut(): pl.pallas_call(functools.partial(cut_kernel, part), grid=(rows // 8,), in...]
    all_to_all x1, waiting for transfers between devices: 3.09 us -> 0.01 us  [exchange(): return lax.all_to_all(value, axes, split_axis=0, concat_axis=0, tiled=True)]
  transfers between devices with their start and end apart: 3 -> 3, of which waited for: 2 -> 1; matrix products, arithmetic and copies ran while one was open for 0% -> 0% of each run, Pallas kernels for 6% -> 9%
where the time goes in v9:
time: 178 us
  blocking collectives  115 us (65%)
  Pallas kernels  36.2 us (20%)
  between operations  13.4 us (8%)
  starting transfers between devices  10.2 us (6%)
  waiting for transfers between devices  1.96 us (1%)
  other arithmetic  1.81 us (1%)
    all_to_all x2, blocking collectives, exchange(): return lax.all_to_all(value, axes, split_axis=0, concat_axis=0, tiled=True)  115 us
    pallas_call x1, Pallas kernels, ladder(): pl.pallas_call(functools.partial(ladder_kernel, part, step), in_specs=[sc...  18.1 us
    pallas_call x1, Pallas kernels, cut(): pl.pallas_call(functools.partial(cut_kernel, part), grid=(rows // 8,), in...  15.7 us
    all_to_all x1, starting transfers between devices, exchange(): return lax.all_to_all(value, axes, split_axis=0, concat_axis=0, tiled=True)  7.63 us
  transfers between devices with their start and end apart: 3, of which 1 were waited for; matrix products, arithmetic and copies ran while one was open for 0% of the time, Pallas kernels for 9%

profile of v9, /device:TPU:1, one launch (start us, length us, event | category | flops | bytes accessed | tf_op | source)
XLA Modules:
  0.0 178.2 jit_solution(5222956163853900317)
XLA Ops:
  6.5 2.4 %shard_map.55 = f32[16,56,256]{2,1,0:T(8,128)} custom-call(s32[1,128]{1,0:T(1,128)} %bitcast.10, s32[1,64]{1,0:T(1,128)} %bitcast.11, s32[1,64]{1,0:T(1,128)} %bitcast.12, f32[800,256]{1,0:T(8,128)} %bitcast.9), custom_call_target="tpu_custom_call" | custom-call | bytes 1638400 | tf_op jit(solution)/shard_map/pallas_call | solution.py:49
  8.9 7.6 %all-to-all-start = ((f32[16,56,256]{2,1,0:T(8,128)}), f32[16,56,256]{2,1,0:T(8,128)}, u32[]{:S(2)}, u32[]{:S(2)}) async-start(f32[16,56,256]{2,1,0:T(8,128)} %shard_map.55), calls=%async_computation | async-start | bytes 1835008 | tf_op jit(solution)/shard_map/all_to_all | solution.py:268
  16.5 0.0 all-gather.3.cloned.1.call-start
  16.6 15.7 %shard_map.56 = f32[16,40,3200]{2,1,0:T(8,128)} custom-call(f32[64,40,800]{2,1,0:T(8,128)} %v_ref.1), custom_call_target="tpu_custom_call" | custom-call | bytes 16384000 | tf_op jit(solution)/shard_map/pallas_call | solution.py:91
  32.3 0.0 all-to-all-done
  32.3 0.0 all-gather.3.cloned.1.call-update
  32.3 99.6 %all_to_all.15.v_hbm = f32[16,40,3200]{2,1,0:T(8,128)} all-to-all(f32[16,40,3200]{2,1,0:T(8,128)} %shard_map.56), channel_id=1, replica_groups=mesh['y'=4,'z'=8,'x'=4,'slab'=2] {'y','x'}, dimensions={0} | all-to-all | bytes 16384000 | tf_op jit(solution)/shard_map/all_to_all | solution.py:268
  132.0 0.0 all-gather.3.cloned.1.call-done.t_hbm
  132.0 18.1 %shard_map.57 = (f32[16,80,128]{2,1,0:T(8,128)}, f32[16,80,128]{2,1,0:T(8,128)}) custom-call(s32[1]{0:T(128)} %bitcast.5.core_ref, s32[1]{0:T(128)} %bitcast.6.plane_ref, f32[16,40,3200]{2,1,0:T(8,128)} %all_to_all.15.v_hbm, f32[128,56,256]{2,1,0:T(8,128)} %all-gather.3.cloned.1.call-done.t_hbm), custom_call_target="tpu_custom_call" | custom-call | flops 12582912000 | bytes 15532032 | tf_op jit(solution)/shard_map/pallas_call | solution.py:234
  150.1 2.5 %collective-permute-start = (f32[16,80,128]{2,1,0:T(8,128)}, f32[16,80,128]{2,1,0:T(8,128)S(1)}, u32[]{:S(2)}, u32[]{:S(2)}) collective-permute-start(f32[16,80,128]{2,1,0:T(8,128)} %get-tuple-element.26), channel_id=1, source_target_pairs={{0,1},{1,0},{2,3},{3,2},{4,5},{5,4},{6,7},{7,6},{8,9},{9,8},{10,11... | collective-permute-start | bytes 1966088 | tf_op jit(solution)/shard_map/ppermute | solution.py:286
  152.6 1.9 %collective-permute-done = f32[16,80,128]{2,1,0:T(8,128)S(1)} collective-permute-done((f32[16,80,128]{2,1,0:T(8,128)}, f32[16,80,128]{2,1,0:T(8,128)S(1)}, u32[]{:S(2)}, u32[]{:S(2)}) %collective-permute-start) | collective-permute-done | bytes 655392 | tf_op jit(solution)/shard_map/ppermute | solution.py:286
  154.5 1.2 add.3
  155.7 15.0 %all_to_all.16 = f32[16,80,128]{2,1,0:T(8,128)S(1)} all-to-all(f32[16,80,128]{2,1,0:T(8,128)S(1)} %add.3), channel_id=1, replica_groups=mesh['y'=4,'z'=8,'x'=4,'slab'=2] {'y','x'}, dimensions={0} | all-to-all | bytes 1310720 | tf_op jit(solution)/shard_map/all_to_all | solution.py:268
  170.7 0.7 reduce_sum.9
Async XLA Ops:
  8.9 23.4 %all-to-all-start = ((f32[16,56,256]{2,1,0:T(8,128)}), f32[16,56,256]{2,1,0:T(8,128)}, u32[]{:S(2)}, u32[]{:S(2)}) async-start(f32[16,56,256]{2,1,0:T(8,128)} %shard_map.55), calls=%async_computation | async-start | bytes 1835008 | tf_op jit(solution)/shard_map/all_to_all | solution.py:268
  16.5 115.4 %all-gather.3.cloned.1.call-start = ((), (), s32[]{:S(2)}) async-start(), calls=%async_computation.3 | async-start | bytes 8257536 | tf_op jit(solution)/shard_map/all_gather | solution.py:281
  150.1 4.4 %collective-permute-start = (f32[16,80,128]{2,1,0:T(8,128)}, f32[16,80,128]{2,1,0:T(8,128)S(1)}, u32[]{:S(2)}, u32[]{:S(2)}) collective-permute-start(f32[16,80,128]{2,1,0:T(8,128)} %get-tuple-element.26), channel_id=1, source_target_pairs={{0,1},{1,0},{2,3},{3,2},{4,5},{5,4},{6,7},{7,6},{8,9},{9,8},{10,11... | collective-permute-start | bytes 1966088 | tf_op jit(solution)/shard_map/ppermute | solution.py:286
Sparse Core Ops, SparseCore 0:
  32.5 87.6 all-gather.2
